TPU v7x, 32 devices: a whole 2x2x4 slice. The times are simulated.
32 devices in a mesh: ctx: 16 (over z, y, x), head: 2 (over core).
Axes of the slice: x: 2, y: 2, z: 4, core: 2. Of those that a mesh axis runs over, the one named last changes fastest.
Arguments:
- q_nope: bfloat16 [4096, 8192], P('ctx', 'head'), may hold values from -6 to 6
- q_rope: bfloat16 [4096, 4096], P('ctx', 'head'), may hold values from -64 to 64
- latents: bfloat16 [4096, 512], P(('ctx', 'head')), may hold values from -6 to 6
- rope_keys: bfloat16 [64, 4096], P(None, ('ctx', 'head')), may hold values from -4 to 4
- doc_lengths: int32 [8], replicated, may hold values from 1 to 1792, 4096 in all
- w_key: bfloat16 [512, 8192], P(None, 'head'), may hold values from -0.25 to 0.25
- w_value: bfloat16 [512, 8192], P(None, 'head'), may hold values from -0.25 to 0.25
Outputs:
- attended: bfloat16 [4096, 8192], P('ctx', 'head')
Inputs may be any that keep to these rules, and one draw needn't show every extreme that they name: `doc_lengths`: they sum to 4096.
All inputs are finite; a program needn't handle non-finite values.
Results may differ from a plain program's by a relative error of at most 0.0064.
Values may be sent and summed in bfloat16 or wider, within the bound.
No kernel may reach another device: no remote copies, remote signals or barrier semaphores. Data moves between devices by JAX's collectives and lax.ppermute only.
A program may use at most 256 MiB of HBM per device.

v0:
```python
import math

import jax
import jax.numpy as jnp
from jax import lax
from jax.sharding import PartitionSpec as P

HEAD_DIM = 128
WINDOW = 8


masked_score = -1e30


def from_behind(x, axis, by):
    length = lax.axis_size(axis)
    pairs = [(i, i + by) for i in range(length) if 0 <= i + by < length]
    return lax.ppermute(x, axis, pairs)


def segment_of(positions, doc_starts):
    return jnp.sum((doc_starts[None, :] <= positions[:, None]).astype(jnp.int32), axis=1) - 1


def circulate(main_part, rope_part):
    arrived = [(main_part, rope_part)]
    current_main, current_rope = (main_part, rope_part)
    for block in range(1, WINDOW):
        current_main, current_rope = from_behind((current_main, current_rope), "ctx", 1)
        arrived.append((current_main, current_rope))
    return arrived


def shards(q_nope, q_rope, latents, rope_keys, doc_lengths, w_key, w_value):
    tok_rows = q_nope.shape[0]
    head_count = q_nope.shape[1] // HEAD_DIM
    rope_width = q_rope.shape[1] // head_count
    score_scale = 1.0 / math.sqrt(HEAD_DIM + rope_width)
    doc_starts = jnp.cumsum(doc_lengths) - doc_lengths
    ctx_place = lax.axis_index("ctx")
    query_place = ctx_place * tok_rows + jnp.arange(tok_rows, dtype=jnp.int32)
    query_doc = segment_of(query_place, doc_starts)
    query_nope = q_nope.reshape(tok_rows, head_count, HEAD_DIM)
    query_rope = q_rope.reshape(tok_rows, head_count, rope_width)
    own_latents, own_rope = (
        lax.all_gather(latents, "head", axis=0, tiled=True),
        lax.all_gather(rope_keys, "head", axis=1, tiled=True),
    )
    arrived = circulate(own_latents, own_rope)
    score_blocks = []
    value_blocks = []
    needed_list = []
    for block in range(WINDOW):
        main_block, rope_block = arrived[block]
        key_place = (ctx_place - block) * tok_rows + jnp.arange(tok_rows, dtype=jnp.int32)
        needed = jnp.logical_or(
            segment_of(key_place[-1:], doc_starts)[0] == query_doc[0], block == 0
        )
        key_rows = jnp.dot(main_block, w_key, preferred_element_type=jnp.float32).astype(
            jnp.bfloat16
        )
        value_rows = jnp.dot(main_block, w_value, preferred_element_type=jnp.float32).astype(
            jnp.bfloat16
        )
        tile_value_rows = value_rows
        scores = jnp.einsum(
            "qhd,khd->qhk",
            query_nope,
            key_rows.reshape(tok_rows, head_count, HEAD_DIM),
            preferred_element_type=jnp.float32,
        )
        scores = scores + jnp.einsum(
            "qhr,rk->qhk", query_rope, rope_block, preferred_element_type=jnp.float32
        )
        scores = scores * score_scale
        visible = (segment_of(key_place, doc_starts)[None, :] == query_doc[:, None]) & (
            key_place[None, :] <= query_place[:, None]
        )
        scores = jnp.where(visible[:, None, :], scores, masked_score)
        scores, value_rows = (scores, tile_value_rows)
        score_blocks.append(scores)
        value_blocks.append(value_rows)
        needed_list.append(needed)
    all_scores = jnp.concatenate(score_blocks, axis=2)
    row_top = jnp.max(all_scores, axis=2, keepdims=True)
    raised = jnp.exp(all_scores - row_top)
    denom_sum = jnp.sum(raised, axis=2)
    weights = raised.astype(jnp.bfloat16)
    mixed_sum = jnp.zeros((tok_rows, head_count, HEAD_DIM), jnp.float32)
    for block in range(WINDOW):
        weight_part = weights[:, :, block * tok_rows : (block + 1) * tok_rows]
        value_part = value_blocks[block].reshape(tok_rows, head_count, HEAD_DIM)
        mixed_sum = mixed_sum + jnp.einsum(
            "qhk,khd->qhd", weight_part, value_part, preferred_element_type=jnp.float32
        )
    return (
        (mixed_sum / denom_sum[:, :, None])
        .astype(jnp.bfloat16)
        .reshape(tok_rows, head_count * HEAD_DIM)
    )


def solution(mesh):
    return jax.shard_map(
        shards,
        mesh=mesh,
        in_specs=(
            P("ctx", "head"),
            P("ctx", "head"),
            P(("ctx", "head"), None),
            P(None, ("ctx", "head")),
            P(),
            P(None, "head"),
            P(None, "head"),
        ),
        out_specs=P("ctx", "head"),
        check_vma=False,
    )
```

profile of v0, /device:TPU:0, one launch (start us, length us, event | category | flops | bytes accessed | tf_op | source)
XLA Modules:
  0.0 370.7 jit_solution(7068967185997697543)
XLA Ops:
  0.0 4.0 %all_gather.6 = bf16[256,512]{1,0:T(8,128)(2,1)} all-gather(bf16[128,512]{1,0:T(8,128)(2,1)} %param.9), channel_id=1, replica_groups=mesh['ctx'=16,'head'=2] {'head'}, dimensions={0}, use_global_device_ids=true | all-gather | bytes 393216 | tf_op jit(solution)/shard_map/all_gather | solution.py:46
  4.0 5.2 %collective-permute-start = (bf16[256,512]{1,0:T(8,128)(2,1)}, bf16[256,512]{1,0:T(8,128)(2,1)}, u32[]{:S(2)}, u32[]{:S(2)}) collective-permute-start(bf16[256,512]{1,0:T(8,128)(2,1)} %all_gather.6), channel_id=1, source_target_pairs={{0,2},{2,4},{4,6},{6,8},{8,10},{10,12},{12,14},{14,16},{16,18},{18... | collective-permute-start | bytes 786440 | tf_op jit(solution)/shard_map/ppermute | solution.py:18
  11.3 2.7 collective-permute-start.1
  15.7 3.5 fusion.67
  19.3 4.4 %fusion.63 = f32[32,256,256]{2,1,0:T(8,128)} fusion(bf16[32,32,8,128]{3,2,1,0:T(8,128)(2,1)S(1)} %fusion.67, bf16[256,4096]{1,0:T(8,128)(2,1)S(1)} %copy-done), kind=kOutput, calls=%fused_computation.89 | convolution fusion | flops 536870912 | bytes 12582912 | tf_op jit(solution)/shard_map/qhd,khd->qhk/dot_general | solution.py:66
  23.8 3.4 collective-permute-start.3
  28.8 4.8 %collective-permute-start.5 = (bf16[64,256]{1,0:T(8,128)(2,1)S(1)}, bf16[64,256]{1,0:T(8,128)(2,1)}, u32[]{:S(2)}, u32[]{:S(2)}) collective-permute-start(bf16[64,256]{1,0:T(8,128)(2,1)S(1)} %collective-permute-done.3), channel_id=1, source_target_pairs={{0,2},{2,4},{4,6},{6,8},{8,10},{10,12},{12,14},{14,16},{16,18},{18... | collective-permute-start | bytes 98312 | tf_op jit(solution)/shard_map/ppermute | solution.py:18
  34.6 4.9 %collective-permute-start.7 = (bf16[64,256]{1,0:T(8,128)(2,1)}, bf16[64,256]{1,0:T(8,128)(2,1)}, u32[]{:S(2)}, u32[]{:S(2)}) collective-permute-start(bf16[64,256]{1,0:T(8,128)(2,1)} %collective-permute-done.5), channel_id=1, source_target_pairs={{0,2},{2,4},{4,6},{6,8},{8,10},{10,12},{12,14},{14,16},{16,18},{18... | collective-permute-start | bytes 98312 | tf_op jit(solution)/shard_map/ppermute | solution.py:18
  42.3 5.3 %collective-permute-start.9 = (bf16[64,256]{1,0:T(8,128)(2,1)}, bf16[64,256]{1,0:T(8,128)(2,1)}, u32[]{:S(2)}, u32[]{:S(2)}) collective-permute-start(bf16[64,256]{1,0:T(8,128)(2,1)} %collective-permute-done.7), channel_id=1, source_target_pairs={{0,2},{2,4},{4,6},{6,8},{8,10},{10,12},{12,14},{14,16},{16,18},{18... | collective-permute-start | bytes 98312 | tf_op jit(solution)/shard_map/ppermute | solution.py:18
  47.6 11.3 %constant_dynamic-update-slice_fusion.7 = (f32[256,32,2048]{0,2,1:T(8,128)}, f32[256,32,256]{0,2,1:T(8,128)}) fusion(bf16[256,32,64]{0,2,1:T(8,128)(2,1)S(1)} %bitcast.235, bf16[64,256]{1,0:T(8,128)(2,1)} %copy-done.10, f32[32,256,256]{2,1,0:T(8,128)} %fusion.63, pred[256,256]{0,1:T(8,128)(4,1)} %get-tuple-element.21), kind=kOutput, calls=%fused_computation.133 | convolution fusion | flops 274726912 | bytes 26312704 | tf_op jit(solution)/shard_map/qhr,rk->qhk/dot_general | solution.py:72
  58.8 4.1 %collective-permute-start.11 = (bf16[64,256]{1,0:T(8,128)(2,1)}, bf16[64,256]{1,0:T(8,128)(2,1)}, u32[]{:S(2)}, u32[]{:S(2)}) collective-permute-start(bf16[64,256]{1,0:T(8,128)(2,1)} %collective-permute-done.9), channel_id=1, source_target_pairs={{0,2},{2,4},{4,6},{6,8},{8,10},{10,12},{12,14},{14,16},{16,18},{18... | collective-permute-start | bytes 98312 | tf_op jit(solution)/shard_map/ppermute | solution.py:18
  63.0 3.6 convolution_convert_fusion.15
  66.6 4.1 %copy.125 = bf16[256,4096]{0,1:T(8,128)(2,1)} copy(bf16[256,4096]{1,0:T(8,128)(2,1)} %convolution_convert_fusion.15) | data formatting | bytes 4194304 | tf_op jit(solution)/shard_map/reshape | solution.py:92
  70.6 4.7 %reduce_max.86 = f32[256,32]{0,1:T(8,128)} reduce(f32[256,32,256]{0,2,1:T(8,128)} %get-tuple-element.24, f32[]{:T(128)} %constant.49.clone.1), dimensions={2}, to_apply=%region_9.10 | reduce | flops 2088960 | bytes 8421380 | tf_op jit(solution)/shard_map/reduce_max | solution.py:85
  75.3 4.9 %collective-permute-start.13 = (bf16[64,256]{1,0:T(8,128)(2,1)}, bf16[64,256]{1,0:T(8,128)(2,1)}, u32[]{:S(2)}, u32[]{:S(2)}) collective-permute-start(bf16[64,256]{1,0:T(8,128)(2,1)} %collective-permute-done.11), channel_id=1, source_target_pairs={{0,2},{2,4},{4,6},{6,8},{8,10},{10,12},{12,14},{14,16},{16,18},{18... | collective-permute-start | bytes 98312 | tf_op jit(solution)/shard_map/ppermute | solution.py:18
  80.3 3.6 fusion.68
  85.1 7.7 %constant_dynamic-update-slice_fusion.6 = (f32[256,32,2048]{0,2,1:T(8,128)}, f32[256,32,256]{0,2,1:T(8,128)}) fusion(f32[256,32,2048]{0,2,1:T(8,128)} %get-tuple-element.23, bf16[256,32,64]{0,2,1:T(8,128)(2,1)S(1)} %bitcast.236, bf16[64,256]{1,0:T(8,128)(2,1)S(1)} %copy-done.12, f32[32,256,256]{2,1,0:T(8,128)S(1)} %fusion.53, ...), kind=kOutput, calls=%fused_computation.132 | convolution fusion | flops 274726912 | bytes 26312704 | tf_op jit(solution)/shard_map/qhr,rk->qhk/dot_general | solution.py:72
  92.8 4.7 %reduce_max.87 = f32[256,32]{0,1:T(8,128)} reduce(f32[256,32,256]{0,2,1:T(8,128)} %get-tuple-element.26, f32[]{:T(128)} %constant.49.clone.1), dimensions={2}, to_apply=%region_10.11 | reduce | flops 2088960 | bytes 8421380 | tf_op jit(solution)/shard_map/reduce_max | solution.py:85
  97.5 5.2 %collective-permute-start.2 = (bf16[256,512]{1,0:T(8,128)(2,1)}, bf16[256,512]{1,0:T(8,128)(2,1)}, u32[]{:S(2)}, u32[]{:S(2)}) collective-permute-start(bf16[256,512]{1,0:T(8,128)(2,1)} %collective-permute-done), channel_id=1, source_target_pairs={{0,2},{2,4},{4,6},{6,8},{8,10},{10,12},{12,14},{14,16},{16,18},{18... | collective-permute-start | bytes 786440 | tf_op jit(solution)/shard_map/ppermute | solution.py:18
  102.7 4.9 %convolution_convert_fusion.6 = bf16[256,4096]{1,0:T(8,128)(2,1)} fusion(bf16[256,512]{1,0:T(8,128)(2,1)} %collective-permute-done, bf16[512,4096]{1,0:T(8,128)(2,1)} %param.13), kind=kOutput, calls=%fused_computation.33 | convolution fusion | flops 1074790400 | bytes 6553600 | tf_op jit(solution)/shard_map/dot_general | solution.py:62
  107.5 4.1 %copy.126 = bf16[256,4096]{0,1:T(8,128)(2,1)} copy(bf16[256,4096]{1,0:T(8,128)(2,1)} %convolution_convert_fusion.6) | data formatting | bytes 4194304 | tf_op jit(solution)/shard_map/reshape | solution.py:92
  111.6 3.5 fusion.69
  116.4 7.5 %constant_dynamic-update-slice_fusion.5 = (f32[256,32,2048]{0,2,1:T(8,128)}, f32[256,32,256]{0,2,1:T(8,128)}) fusion(f32[256,32,2048]{0,2,1:T(8,128)} %get-tuple-element.25, bf16[256,32,64]{0,2,1:T(8,128)(2,1)S(1)} %bitcast.237, bf16[64,256]{1,0:T(8,128)(2,1)S(1)} %copy-done.14, f32[32,256,256]{2,1,0:T(8,128)S(1)} %fusion.50, ...), kind=kOutput, calls=%fused_computation.131 | convolution fusion | flops 274726912 | bytes 26312704 | tf_op jit(solution)/shard_map/qhr,rk->qhk/dot_general | solution.py:72
  124.0 4.1 %reduce_max.89 = f32[256,32]{0,1:T(8,128)S(1)} reduce(f32[256,32,256]{0,2,1:T(8,128)} %get-tuple-element.28, f32[]{:T(128)} %constant.49.clone.1), dimensions={2}, to_apply=%region_11.12 | reduce | flops 2088960 | bytes 8421380 | tf_op jit(solution)/shard_map/reduce_max | solution.py:85
  128.1 2.2 collective-permute-start.4
  130.2 4.9 %convolution_convert_fusion.5 = bf16[256,4096]{1,0:T(8,128)(2,1)} fusion(bf16[256,512]{1,0:T(8,128)(2,1)} %collective-permute-done.2, bf16[512,4096]{1,0:T(8,128)(2,1)} %param.13), kind=kOutput, calls=%fused_computation.32 | convolution fusion | flops 1074790400 | bytes 6553600 | tf_op jit(solution)/shard_map/dot_general | solution.py:62
  135.1 4.1 %copy.127 = bf16[256,4096]{0,1:T(8,128)(2,1)} copy(bf16[256,4096]{1,0:T(8,128)(2,1)} %convolution_convert_fusion.5) | data formatting | bytes 4194304 | tf_op jit(solution)/shard_map/reshape | solution.py:92
  139.2 3.5 fusion.70
  144.0 8.3 %constant_dynamic-update-slice_fusion.4 = (f32[256,32,2048]{0,2,1:T(8,128)}, f32[256,32,256]{0,2,1:T(8,128)}) fusion(f32[256,32,2048]{0,2,1:T(8,128)} %get-tuple-element.27, bf16[256,32,64]{0,2,1:T(8,128)(2,1)S(1)} %bitcast.238, bf16[64,256]{1,0:T(8,128)(2,1)} %collective-permute-done.5, f32[32,256,256]{2,1,0:T(8,128)S(1)} %fusion.47, ...), kind=kOutput, calls=%fused_computation.130 | convolution fusion | flops 274726912 | bytes 26312704 | tf_op jit(solution)/shard_map/qhr,rk->qhk/dot_general | solution.py:72
  152.3 4.1 %reduce_max.91 = f32[256,32]{0,1:T(8,128)S(1)} reduce(f32[256,32,256]{0,2,1:T(8,128)} %get-tuple-element.30, f32[]{:T(128)} %constant.49.clone.1), dimensions={2}, to_apply=%region_12.13 | reduce | flops 2088960 | bytes 8421380 | tf_op jit(solution)/shard_map/reduce_max | solution.py:85
  158.6 4.9 %convolution_convert_fusion.4 = bf16[256,4096]{1,0:T(8,128)(2,1)} fusion(bf16[256,512]{1,0:T(8,128)(2,1)} %collective-permute-done.4, bf16[512,4096]{1,0:T(8,128)(2,1)} %param.13), kind=kOutput, calls=%fused_computation.31 | convolution fusion | flops 1074790400 | bytes 6553600 | tf_op jit(solution)/shard_map/dot_general | solution.py:62
  163.4 4.1 %copy.128 = bf16[256,4096]{0,1:T(8,128)(2,1)} copy(bf16[256,4096]{1,0:T(8,128)(2,1)} %convolution_convert_fusion.4) | data formatting | bytes 4194304 | tf_op jit(solution)/shard_map/reshape | solution.py:92
  167.5 3.5 fusion.71
  172.3 8.3 %constant_dynamic-update-slice_fusion.3 = (f32[256,32,2048]{0,2,1:T(8,128)}, f32[256,32,256]{0,2,1:T(8,128)}) fusion(f32[256,32,2048]{0,2,1:T(8,128)} %get-tuple-element.29, bf16[256,32,64]{0,2,1:T(8,128)(2,1)S(1)} %bitcast.239, bf16[64,256]{1,0:T(8,128)(2,1)} %collective-permute-done.7, f32[32,256,256]{2,1,0:T(8,128)S(1)} %fusion.44, ...), kind=kOutput, calls=%fused_computation.129 | convolution fusion | flops 274726912 | bytes 26312704 | tf_op jit(solution)/shard_map/qhr,rk->qhk/dot_general | solution.py:72
  180.6 4.1 %reduce_max.93 = f32[256,32]{0,1:T(8,128)S(1)} reduce(f32[256,32,256]{0,2,1:T(8,128)} %get-tuple-element.32, f32[]{:T(128)} %constant.49.clone.1), dimensions={2}, to_apply=%region_13.14 | reduce | flops 2088960 | bytes 8421380 | tf_op jit(solution)/shard_map/reduce_max | solution.py:85
  184.7 4.8 %collective-permute-start.8 = (bf16[256,512]{1,0:T(8,128)(2,1)}, bf16[256,512]{1,0:T(8,128)(2,1)}, u32[]{:S(2)}, u32[]{:S(2)}) collective-permute-start(bf16[256,512]{1,0:T(8,128)(2,1)} %collective-permute-done.6), channel_id=1, source_target_pairs={{0,2},{2,4},{4,6},{6,8},{8,10},{10,12},{12,14},{14,16},{16,18},{18... | collective-permute-start | bytes 786440 | tf_op jit(solution)/shard_map/ppermute | solution.py:18
  189.6 4.9 %convolution_convert_fusion.3 = bf16[256,4096]{1,0:T(8,128)(2,1)} fusion(bf16[256,512]{1,0:T(8,128)(2,1)} %collective-permute-done.6, bf16[512,4096]{1,0:T(8,128)(2,1)} %param.13), kind=kOutput, calls=%fused_computation.30 | convolution fusion | flops 1074790400 | bytes 6553600 | tf_op jit(solution)/shard_map/dot_general | solution.py:62
  194.5 4.1 %copy.129 = bf16[256,4096]{0,1:T(8,128)(2,1)} copy(bf16[256,4096]{1,0:T(8,128)(2,1)} %convolution_convert_fusion.3) | data formatting | bytes 4194304 | tf_op jit(solution)/shard_map/reshape | solution.py:92
  198.5 3.5 fusion.72
  203.4 8.3 %constant_dynamic-update-slice_fusion.2 = (f32[256,32,2048]{0,2,1:T(8,128)}, f32[256,32,256]{0,2,1:T(8,128)}) fusion(f32[256,32,2048]{0,2,1:T(8,128)} %get-tuple-element.31, bf16[256,32,64]{0,2,1:T(8,128)(2,1)S(1)} %bitcast.240, bf16[64,256]{1,0:T(8,128)(2,1)} %collective-permute-done.9, f32[32,256,256]{2,1,0:T(8,128)S(1)} %fusion.41, ...), kind=kOutput, calls=%fused_computation.128 | convolution fusion | flops 274726912 | bytes 26312704 | tf_op jit(solution)/shard_map/qhr,rk->qhk/dot_general | solution.py:72
  211.7 4.1 %reduce_max.95 = f32[256,32]{0,1:T(8,128)S(1)} reduce(f32[256,32,256]{0,2,1:T(8,128)} %get-tuple-element.34, f32[]{:T(128)} %constant.49.clone.1), dimensions={2}, to_apply=%region_14.15 | reduce | flops 2088960 | bytes 8421380 | tf_op jit(solution)/shard_map/reduce_max | solution.py:85
  215.8 5.1 %collective-permute-start.10 = (bf16[256,512]{1,0:T(8,128)(2,1)}, bf16[256,512]{1,0:T(8,128)(2,1)}, u32[]{:S(2)}, u32[]{:S(2)}) collective-permute-start(bf16[256,512]{1,0:T(8,128)(2,1)} %collective-permute-done.8), channel_id=1, source_target_pairs={{0,2},{2,4},{4,6},{6,8},{8,10},{10,12},{12,14},{14,16},{16,18},{18... | collective-permute-start | bytes 786440 | tf_op jit(solution)/shard_map/ppermute | solution.py:18
  220.9 4.9 %convolution_convert_fusion.2 = bf16[256,4096]{1,0:T(8,128)(2,1)} fusion(bf16[256,512]{1,0:T(8,128)(2,1)} %collective-permute-done.8, bf16[512,4096]{1,0:T(8,128)(2,1)} %param.13), kind=kOutput, calls=%fused_computation.29 | convolution fusion | flops 1074790400 | bytes 6553600 | tf_op jit(solution)/shard_map/dot_general | solution.py:62
  225.7 4.1 %copy.130 = bf16[256,4096]{0,1:T(8,128)(2,1)} copy(bf16[256,4096]{1,0:T(8,128)(2,1)} %convolution_convert_fusion.2) | data formatting | bytes 4194304 | tf_op jit(solution)/shard_map/reshape | solution.py:92
  229.8 3.5 fusion.73
  234.6 8.4 %constant_dynamic-update-slice_fusion.1 = (f32[256,32,2048]{0,2,1:T(8,128)}, f32[256,32,256]{0,2,1:T(8,128)}) fusion(f32[256,32,2048]{0,2,1:T(8,128)} %get-tuple-element.33, bf16[256,32,64]{0,2,1:T(8,128)(2,1)S(1)} %bitcast.241, bf16[64,256]{1,0:T(8,128)(2,1)} %collective-permute-done.11, f32[32,256,256]{2,1,0:T(8,128)S(1)} %fusion.38, ...), kind=kOutput, calls=%fused_computation.127 | convolution fusion | flops 274726912 | bytes 26312704 | tf_op jit(solution)/shard_map/qhr,rk->qhk/dot_general | solution.py:72
  243.0 4.1 %reduce_max.97 = f32[256,32]{0,1:T(8,128)S(1)} reduce(f32[256,32,256]{0,2,1:T(8,128)} %get-tuple-element.36, f32[]{:T(128)} %constant.49.clone.1), dimensions={2}, to_apply=%region_15.16 | reduce | flops 2088960 | bytes 8421380 | tf_op jit(solution)/shard_map/reduce_max | solution.py:85
  249.3 4.9 %convolution_convert_fusion.1 = bf16[256,4096]{1,0:T(8,128)(2,1)} fusion(bf16[256,512]{1,0:T(8,128)(2,1)} %collective-permute-done.10, bf16[512,4096]{1,0:T(8,128)(2,1)} %param.13), kind=kOutput, calls=%fused_computation.28 | convolution fusion | flops 1074790400 | bytes 6553600 | tf_op jit(solution)/shard_map/dot_general | solution.py:62
  254.2 4.1 %copy.131 = bf16[256,4096]{0,1:T(8,128)(2,1)} copy(bf16[256,4096]{1,0:T(8,128)(2,1)} %convolution_convert_fusion.1) | data formatting | bytes 4194304 | tf_op jit(solution)/shard_map/reshape | solution.py:92
  258.3 3.5 fusion.74
  263.1 8.4 %constant_dynamic-update-slice_fusion = (f32[256,32,2048]{0,2,1:T(8,128)}, f32[256,32,256]{0,2,1:T(8,128)}) fusion(f32[256,32,2048]{0,2,1:T(8,128)} %get-tuple-element.35, bf16[256,32,64]{0,2,1:T(8,128)(2,1)S(1)} %bitcast.242, bf16[64,256]{1,0:T(8,128)(2,1)} %collective-permute-done.13, f32[32,256,256]{2,1,0:T(8,128)S(1)} %fusion.35, ...), kind=kOutput, calls=%fused_computation.126 | convolution fusion | flops 274726912 | bytes 26312704 | tf_op jit(solution)/shard_map/qhr,rk->qhk/dot_general | solution.py:72
  271.5 4.1 %reduce_max.99 = f32[256,32]{0,1:T(8,128)S(1)} reduce(f32[256,32,256]{0,2,1:T(8,128)} %get-tuple-element.38, f32[]{:T(128)} %constant.49.clone.1), dimensions={2}, to_apply=%region_16.17 | reduce | flops 2088960 | bytes 8421380 | tf_op jit(solution)/shard_map/reduce_max | solution.py:85
  275.7 32.9 %fusion = (f32[256,32]{0,1:T(8,128)S(1)}, bf16[256,32,2048]{0,2,1:T(8,128)(2,1)}) fusion(f32[256,32,2048]{0,2,1:T(8,128)} %get-tuple-element.37, f32[256,32]{0,1:T(8,128)S(1)} %maximum_maximum_fusion), kind=kLoop, calls=%fused_computation.1 | loop fusion | flops 50323456 | bytes 100728832 | tf_op jit(solution)/shard_map/reduce_sum | solution.py:87
  308.6 5.6 %fusion.22 = f32[32,128,256]{2,1,0:T(8,128)} fusion(bf16[256,32,128]{0,2,1:T(8,128)(2,1)} %bitcast.248, bf16[256,32,2048]{0,2,1:T(8,128)(2,1)} %get-tuple-element.14), kind=kOutput, calls=%fused_computation.47 | convolution fusion | flops 536870912 | bytes 10485760 | tf_op jit(solution)/shard_map/qhk,khd->qhd/dot_general | solution.py:93
  314.2 5.0 %fusion.24 = f32[32,128,256]{2,1,0:T(8,128)} fusion(bf16[256,32,128]{0,2,1:T(8,128)(2,1)S(1)} %bitcast.247, bf16[256,32,2048]{0,2,1:T(8,128)(2,1)} %get-tuple-element.14), kind=kOutput, calls=%fused_computation.49 | convolution fusion | flops 536870912 | bytes 10485760 | tf_op jit(solution)/shard_map/qhk,khd->qhd/dot_general | solution.py:93
  319.3 5.0 %fusion.26 = f32[32,128,256]{2,1,0:T(8,128)} fusion(bf16[256,32,128]{0,2,1:T(8,128)(2,1)S(1)} %bitcast.246, bf16[256,32,2048]{0,2,1:T(8,128)(2,1)} %get-tuple-element.14), kind=kOutput, calls=%fused_computation.51 | convolution fusion | flops 536870912 | bytes 10485760 | tf_op jit(solution)/shard_map/qhk,khd->qhd/dot_general | solution.py:93
  324.3 5.0 %fusion.28 = f32[32,128,256]{2,1,0:T(8,128)} fusion(bf16[256,32,128]{0,2,1:T(8,128)(2,1)S(1)} %bitcast.245, bf16[256,32,2048]{0,2,1:T(8,128)(2,1)} %get-tuple-element.14), kind=kOutput, calls=%fused_computation.53 | convolution fusion | flops 536870912 | bytes 10485760 | tf_op jit(solution)/shard_map/qhk,khd->qhd/dot_general | solution.py:93
  329.3 5.0 %fusion.30 = f32[32,128,256]{2,1,0:T(8,128)} fusion(bf16[256,32,128]{0,2,1:T(8,128)(2,1)S(1)} %bitcast.244, bf16[256,32,2048]{0,2,1:T(8,128)(2,1)} %get-tuple-element.14), kind=kOutput, calls=%fused_computation.55 | convolution fusion | flops 536870912 | bytes 10485760 | tf_op jit(solution)/shard_map/qhk,khd->qhd/dot_general | solution.py:93
  334.3 5.0 %fusion.32 = f32[32,128,256]{2,1,0:T(8,128)} fusion(bf16[256,32,128]{0,2,1:T(8,128)(2,1)S(1)} %bitcast.243, bf16[256,32,2048]{0,2,1:T(8,128)(2,1)} %get-tuple-element.14), kind=kOutput, calls=%fused_computation.57 | convolution fusion | flops 536870912 | bytes 10485760 | tf_op jit(solution)/shard_map/qhk,khd->qhd/dot_general | solution.py:93
  339.3 5.0 %fusion.20 = f32[32,128,256]{2,1,0:T(8,128)} fusion(bf16[256,32,128]{0,2,1:T(8,128)(2,1)S(1)} %bitcast.249, bf16[256,32,2048]{0,2,1:T(8,128)(2,1)} %get-tuple-element.14), kind=kOutput, calls=%fused_computation.45 | convolution fusion | flops 536870912 | bytes 10485760 | tf_op jit(solution)/shard_map/qhk,khd->qhd/dot_general | solution.py:93
  344.4 3.5 convolution_convert_fusion
  347.9 4.1 %copy.132 = bf16[256,4096]{0,1:T(8,128)(2,1)} copy(bf16[256,4096]{1,0:T(8,128)(2,1)} %convolution_convert_fusion) | data formatting | bytes 4194304 | tf_op jit(solution)/shard_map/reshape | solution.py:92
  352.0 14.5 %fusion.34 = bf16[256,32,128]{0,2,1:T(8,128)(2,1)} fusion(f32[32,128,256]{2,1,0:T(8,128)} %fusion.20, f32[32,128,256]{2,1,0:T(8,128)} %fusion.22, f32[32,128,256]{2,1,0:T(8,128)} %fusion.24, f32[32,128,256]{2,1,0:T(8,128)} %fusion.26, f32[32,128,256]{2,1,0:T(8,128)} %fusion.28, f32[32,128,256]{2,1,0:T(8,128)} %fusion.32, f32[32,128,256]{2,1,0:T(8,128)} %fusion.30, ...), kind=kOutput, calls=%fused_computation.60 | convolution fusion | flops 546308096 | bytes 37781504 | tf_op jit(solution)/shard_map/qhk,khd->qhd/dot_general | solution.py:93
  366.5 4.1 %copy.116 = bf16[256,4096]{1,0:T(8,128)(2,1)} copy(bf16[256,4096]{0,1:T(8,128)(2,1)} %bitcast.251) | data formatting | bytes 4194304 | tf_op jit(solution)/shard_map/reshape | solution.py:99
  (76 shorter events, 22.3 us)
Async XLA Ops:
  0.0 19.3 %copy-start = (bf16[256,4096]{1,0:T(8,128)(2,1)S(1)}, bf16[256,4096]{1,0:T(8,128)(2,1)}, u32[]{:S(2)}) copy-start(bf16[256,4096]{1,0:T(8,128)(2,1)} %param.7) | copy-start | bytes 6291460
  4.0 76.3 %collective-permute-start = (bf16[256,512]{1,0:T(8,128)(2,1)}, bf16[256,512]{1,0:T(8,128)(2,1)}, u32[]{:S(2)}, u32[]{:S(2)}) collective-permute-start(bf16[256,512]{1,0:T(8,128)(2,1)} %all_gather.6), channel_id=1, source_target_pairs={{0,2},{2,4},{4,6},{6,8},{8,10},{10,12},{12,14},{14,16},{16,18},{18... | collective-permute-start | bytes 786440 | tf_op jit(solution)/shard_map/ppermute | solution.py:18
  11.3 7.9 %copy-start.10 = (bf16[64,256]{1,0:T(8,128)(2,1)}, bf16[64,256]{1,0:T(8,128)(2,1)S(1)}, u32[]{:S(2)}) copy-start(bf16[64,256]{1,0:T(8,128)(2,1)S(1)} %all_gather.7) | copy-start | bytes 98308
  11.3 12.5 %collective-permute-start.1 = (bf16[64,256]{1,0:T(8,128)(2,1)S(1)}, bf16[64,256]{1,0:T(8,128)(2,1)S(1)}, u32[]{:S(2)}, u32[]{:S(2)}) collective-permute-start(bf16[64,256]{1,0:T(8,128)(2,1)S(1)} %all_gather.7), channel_id=1, source_target_pairs={{0,2},{2,4},{4,6},{6,8},{8,10},{10,12},{12,14},{14,16},{16,18},{18... | collective-permute-start | bytes 98312 | tf_op jit(solution)/shard_map/ppermute | solution.py:18
  23.8 15.7 %copy-start.11 = (bf16[64,256]{1,0:T(8,128)(2,1)}, bf16[64,256]{1,0:T(8,128)(2,1)S(1)}, u32[]{:S(2)}) copy-start(bf16[64,256]{1,0:T(8,128)(2,1)S(1)} %collective-permute-done.1) | copy-start | bytes 98308
  23.8 5.0 %collective-permute-start.3 = (bf16[64,256]{1,0:T(8,128)(2,1)S(1)}, bf16[64,256]{1,0:T(8,128)(2,1)S(1)}, u32[]{:S(2)}, u32[]{:S(2)}) collective-permute-start(bf16[64,256]{1,0:T(8,128)(2,1)S(1)} %collective-permute-done.1), channel_id=1, source_target_pairs={{0,2},{2,4},{4,6},{6,8},{8,10},{10,12},{12,14},{14,16},{16,18},{18... | collective-permute-start | bytes 98312 | tf_op jit(solution)/shard_map/ppermute | solution.py:18
  28.8 10.7 %copy-start.13 = (bf16[64,256]{1,0:T(8,128)(2,1)}, bf16[64,256]{1,0:T(8,128)(2,1)S(1)}, u32[]{:S(2)}) copy-start(bf16[64,256]{1,0:T(8,128)(2,1)S(1)} %collective-permute-done.3) | copy-start | bytes 98308
  28.8 5.8 %collective-permute-start.5 = (bf16[64,256]{1,0:T(8,128)(2,1)S(1)}, bf16[64,256]{1,0:T(8,128)(2,1)}, u32[]{:S(2)}, u32[]{:S(2)}) collective-permute-start(bf16[64,256]{1,0:T(8,128)(2,1)S(1)} %collective-permute-done.3), channel_id=1, source_target_pairs={{0,2},{2,4},{4,6},{6,8},{8,10},{10,12},{12,14},{14,16},{16,18},{18... | collective-permute-start | bytes 98312 | tf_op jit(solution)/shard_map/ppermute | solution.py:18
  34.6 7.7 %collective-permute-start.7 = (bf16[64,256]{1,0:T(8,128)(2,1)}, bf16[64,256]{1,0:T(8,128)(2,1)}, u32[]{:S(2)}, u32[]{:S(2)}) collective-permute-start(bf16[64,256]{1,0:T(8,128)(2,1)} %collective-permute-done.5), channel_id=1, source_target_pairs={{0,2},{2,4},{4,6},{6,8},{8,10},{10,12},{12,14},{14,16},{16,18},{18... | collective-permute-start | bytes 98312 | tf_op jit(solution)/shard_map/ppermute | solution.py:18
  42.3 16.5 %collective-permute-start.9 = (bf16[64,256]{1,0:T(8,128)(2,1)}, bf16[64,256]{1,0:T(8,128)(2,1)}, u32[]{:S(2)}, u32[]{:S(2)}) collective-permute-start(bf16[64,256]{1,0:T(8,128)(2,1)} %collective-permute-done.7), channel_id=1, source_target_pairs={{0,2},{2,4},{4,6},{6,8},{8,10},{10,12},{12,14},{14,16},{16,18},{18... | collective-permute-start | bytes 98312 | tf_op jit(solution)/shard_map/ppermute | solution.py:18
  47.6 15.4 %copy-start.15 = (bf16[512,4096]{1,0:T(8,128)(2,1)S(1)}, bf16[512,4096]{1,0:T(8,128)(2,1)}, u32[]{:S(2)}) copy-start(bf16[512,4096]{1,0:T(8,128)(2,1)} %param.13) | copy-start | bytes 12582916
  58.8 16.5 %collective-permute-start.11 = (bf16[64,256]{1,0:T(8,128)(2,1)}, bf16[64,256]{1,0:T(8,128)(2,1)}, u32[]{:S(2)}, u32[]{:S(2)}) collective-permute-start(bf16[64,256]{1,0:T(8,128)(2,1)} %collective-permute-done.9), channel_id=1, source_target_pairs={{0,2},{2,4},{4,6},{6,8},{8,10},{10,12},{12,14},{14,16},{16,18},{18... | collective-permute-start | bytes 98312 | tf_op jit(solution)/shard_map/ppermute | solution.py:18
  75.3 187.7 %collective-permute-start.13 = (bf16[64,256]{1,0:T(8,128)(2,1)}, bf16[64,256]{1,0:T(8,128)(2,1)}, u32[]{:S(2)}, u32[]{:S(2)}) collective-permute-start(bf16[64,256]{1,0:T(8,128)(2,1)} %collective-permute-done.11), channel_id=1, source_target_pairs={{0,2},{2,4},{4,6},{6,8},{8,10},{10,12},{12,14},{14,16},{16,18},{18... | collective-permute-start | bytes 98312 | tf_op jit(solution)/shard_map/ppermute | solution.py:18
  83.8 1.3 copy-start.7
  83.8 1.3 copy-start.12
  97.5 14.1 %collective-permute-start.2 = (bf16[256,512]{1,0:T(8,128)(2,1)}, bf16[256,512]{1,0:T(8,128)(2,1)}, u32[]{:S(2)}, u32[]{:S(2)}) collective-permute-start(bf16[256,512]{1,0:T(8,128)(2,1)} %collective-permute-done), channel_id=1, source_target_pairs={{0,2},{2,4},{4,6},{6,8},{8,10},{10,12},{12,14},{14,16},{16,18},{18... | collective-permute-start | bytes 786440 | tf_op jit(solution)/shard_map/ppermute | solution.py:18
  115.2 1.3 copy-start.14
  128.1 11.1 %collective-permute-start.4 = (bf16[256,512]{1,0:T(8,128)(2,1)}, bf16[256,512]{1,0:T(8,128)(2,1)}, u32[]{:S(2)}, u32[]{:S(2)}) collective-permute-start(bf16[256,512]{1,0:T(8,128)(2,1)} %collective-permute-done.2), channel_id=1, source_target_pairs={{0,2},{2,4},{4,6},{6,8},{8,10},{10,12},{12,14},{14,16},{16,18},{18... | collective-permute-start | bytes 786440 | tf_op jit(solution)/shard_map/ppermute | solution.py:18
  156.4 11.1 %collective-permute-start.6 = (bf16[256,512]{1,0:T(8,128)(2,1)}, bf16[256,512]{1,0:T(8,128)(2,1)}, u32[]{:S(2)}, u32[]{:S(2)}) collective-permute-start(bf16[256,512]{1,0:T(8,128)(2,1)} %collective-permute-done.4), channel_id=1, source_target_pairs={{0,2},{2,4},{4,6},{6,8},{8,10},{10,12},{12,14},{14,16},{16,18},{18... | collective-permute-start | bytes 786440 | tf_op jit(solution)/shard_map/ppermute | solution.py:18
  184.7 13.8 %collective-permute-start.8 = (bf16[256,512]{1,0:T(8,128)(2,1)}, bf16[256,512]{1,0:T(8,128)(2,1)}, u32[]{:S(2)}, u32[]{:S(2)}) collective-permute-start(bf16[256,512]{1,0:T(8,128)(2,1)} %collective-permute-done.6), channel_id=1, source_target_pairs={{0,2},{2,4},{4,6},{6,8},{8,10},{10,12},{12,14},{14,16},{16,18},{18... | collective-permute-start | bytes 786440 | tf_op jit(solution)/shard_map/ppermute | solution.py:18
  215.8 14.0 %collective-permute-start.10 = (bf16[256,512]{1,0:T(8,128)(2,1)}, bf16[256,512]{1,0:T(8,128)(2,1)}, u32[]{:S(2)}, u32[]{:S(2)}) collective-permute-start(bf16[256,512]{1,0:T(8,128)(2,1)} %collective-permute-done.8), channel_id=1, source_target_pairs={{0,2},{2,4},{4,6},{6,8},{8,10},{10,12},{12,14},{14,16},{16,18},{18... | collective-permute-start | bytes 786440 | tf_op jit(solution)/shard_map/ppermute | solution.py:18
  247.2 11.1 %collective-permute-start.12 = (bf16[256,512]{1,0:T(8,128)(2,1)}, bf16[256,512]{1,0:T(8,128)(2,1)}, u32[]{:S(2)}, u32[]{:S(2)}) collective-permute-start(bf16[256,512]{1,0:T(8,128)(2,1)} %collective-permute-done.10), channel_id=1, source_target_pairs={{0,2},{2,4},{4,6},{6,8},{8,10},{10,12},{12,14},{14,16},{16,18},{18... | collective-permute-start | bytes 786440 | tf_op jit(solution)/shard_map/ppermute | solution.py:18
  271.5 4.1 %copy-start.8 = (f32[256,32]{0,1:T(8,128)S(1)}, f32[256,32]{0,1:T(8,128)}, u32[]{:S(2)}) copy-start(f32[256,32]{0,1:T(8,128)} %reduce_max.86) | copy-start | bytes 98308
  271.5 4.1 %copy-start.9 = (f32[256,32]{0,1:T(8,128)S(1)}, f32[256,32]{0,1:T(8,128)}, u32[]{:S(2)}) copy-start(f32[256,32]{0,1:T(8,128)} %reduce_max.87) | copy-start | bytes 98308
  308.6 5.6 %copy-start.5 = (bf16[256,4096]{0,1:T(8,128)(2,1)S(1)}, bf16[256,4096]{0,1:T(8,128)(2,1)}, u32[]{:S(2)}) copy-start(bf16[256,4096]{0,1:T(8,128)(2,1)} %copy.129) | copy-start | bytes 6291460
  314.2 5.0 %copy-start.4 = (bf16[256,4096]{0,1:T(8,128)(2,1)S(1)}, bf16[256,4096]{0,1:T(8,128)(2,1)}, u32[]{:S(2)}) copy-start(bf16[256,4096]{0,1:T(8,128)(2,1)} %copy.128) | copy-start | bytes 6291460
  319.3 5.0 %copy-start.3 = (bf16[256,4096]{0,1:T(8,128)(2,1)S(1)}, bf16[256,4096]{0,1:T(8,128)(2,1)}, u32[]{:S(2)}) copy-start(bf16[256,4096]{0,1:T(8,128)(2,1)} %copy.127) | copy-start | bytes 6291460
  324.3 5.0 %copy-start.2 = (bf16[256,4096]{0,1:T(8,128)(2,1)S(1)}, bf16[256,4096]{0,1:T(8,128)(2,1)}, u32[]{:S(2)}) copy-start(bf16[256,4096]{0,1:T(8,128)(2,1)} %copy.126) | copy-start | bytes 6291460
  329.3 5.0 %copy-start.1 = (bf16[256,4096]{0,1:T(8,128)(2,1)S(1)}, bf16[256,4096]{0,1:T(8,128)(2,1)}, u32[]{:S(2)}) copy-start(bf16[256,4096]{0,1:T(8,128)(2,1)} %copy.125) | copy-start | bytes 6291460
  334.3 5.0 %copy-start.6 = (bf16[256,4096]{0,1:T(8,128)(2,1)S(1)}, bf16[256,4096]{0,1:T(8,128)(2,1)}, u32[]{:S(2)}) copy-start(bf16[256,4096]{0,1:T(8,128)(2,1)} %copy.131) | copy-start | bytes 6291460
  339.3 5.0 %copy-start.16 = (bf16[512,4096]{1,0:T(8,128)(2,1)S(1)}, bf16[512,4096]{1,0:T(8,128)(2,1)}, u32[]{:S(2)}) copy-start(bf16[512,4096]{1,0:T(8,128)(2,1)} %param.13) | copy-start | bytes 12582916
where the time goes:
time: 378 us; the launch traced here: 371 us
  matrix products  196 us (52%)
  other arithmetic  70 us (19%)
  starting transfers between devices  56.9 us (15%)
  local copies, waits for them, and re-layouts  38.3 us (10%)
  blocking collectives  6.08 us (2%)
    dot_general x8, matrix products, shards(): jnp.einsum('qhr,rk->qhk', query_rope, rope_block, preferred_element_type=...  68.1 us
    ppermute x14, starting transfers between devices, from_behind(): return lax.ppermute(x, axis, pairs)  56.9 us
    dot_general x8, matrix products, shards(): jnp.einsum('qhk,khd->qhd', weight_part, value_part, preferred_element_typ...  50.3 us
    dot_general x8, matrix products, shards(): jnp.dot(main_block, w_value, preferred_element_type=jnp.float32)  36.3 us
    reduce_max x9, other arithmetic, shards(): row_top = jnp.max(all_scores, axis=2, keepdims=True)  34.1 us
    reduce_sum x1, other arithmetic, shards(): denom_sum = jnp.sum(raised, axis=2)  32.9 us
    reshape x8, local copies, waits for them, and re-layouts, shards(): value_part = value_blocks[block].reshape(tok_rows, head_count, HEAD_DIM)  32.7 us
    dot_general x8, matrix products, shards(): jnp.dot(main_block, w_key, preferred_element_type=jnp.float32)  28.4 us
  transfers between devices with their start and end apart: 14, of which 2 were waited for; matrix products, arithmetic and copies ran while one was open for 53% of the time, Pallas kernels for 0%

commit v1 on v0

v1 whole, which is shorter than its diff:
```python
import functools
import math

import jax
import jax.numpy as jnp
from jax import lax
from jax.experimental import pallas as pl
from jax.experimental.pallas import tpu as pltpu
from jax.sharding import PartitionSpec as P

HEAD_DIM = 128
WINDOW = 8
GROUP = 4

masked_score = -1e30
f32, bf16 = jnp.float32, jnp.bfloat16
NT = (((1,), (1,)), ((), ()))


def from_behind(x, by):
    length = lax.axis_size("ctx")
    return lax.ppermute(x, "ctx", [(i, (i + by) % length) for i in range(length)])


def pack_kernel(latents, rope_keys, packed):
    rows = latents.shape[0]
    packed[:rows, :] = latents[...]
    lanes = rope_keys.shape[1]
    pieces = latents.shape[1] // lanes
    tall = rope_keys.shape[0] // pieces
    for piece in range(pieces):
        packed[rows:, piece * lanes : (piece + 1) * lanes] = rope_keys[
            piece * tall : (piece + 1) * tall, :
        ]


def pack(latents, rope_keys):
    rows, width = latents.shape
    below = rope_keys.size // width
    return pl.pallas_call(
        pack_kernel, out_shape=jax.ShapeDtypeStruct((rows + below, width), bf16)
    )(latents, rope_keys)


def attend_kernel(shape, *refs):
    blocks, parts, first_back, first, last, rope = shape
    lengths, place = refs[:2]
    material = refs[2 : 2 + parts]
    q_nope, q_rope, w_key, w_value = refs[2 + parts : 6 + parts]
    rest = refs[6 + parts :]
    if not first:
        acc_in, stat_in = rest[:2]
        rest = rest[2:]
    if last:
        out = rest[0]
        rest = rest[1:]
    else:
        acc_out, stat_out = rest[:2]
        rest = rest[2:]
    keys, values, side, query_side, *score_and_weight = rest
    score_refs, weight_refs = score_and_weight[:2], score_and_weight[2:]
    tok = q_nope.shape[0]
    span = blocks * tok
    part_rows = tok // parts
    width = w_key.shape[0]
    scale = math.log2(math.e) / math.sqrt(HEAD_DIM + rope)
    lane = lax.broadcasted_iota(jnp.int32, (tok, 128), 1)
    low = lane < 64

    @pl.when(pl.program_id(0) == 0)
    def _():
        at = lax.broadcasted_iota(jnp.int32, (8, 128), 1) % 64
        start, stop = jnp.zeros((8, 128), jnp.int32), jnp.zeros((8, 128), jnp.int32)
        before = jnp.int32(0)
        for doc in range(lengths.shape[0]):
            after = before + lengths[doc]
            start = jnp.where(at == doc, before, start)
            stop = jnp.where(at == doc, after, stop)
            before = after
        start, stop = start[:1], stop[:1]
        row = lax.broadcasted_iota(jnp.int32, (tok, 128), 0)
        position = place[0] * tok + row
        inside = (position >= start) & (position < stop)
        query_side[...] = jnp.where(inside, 1.0, 0.0).astype(bf16)
        for block in range(blocks):
            position = (place[0] - first_back - block) * tok + (row + place[1] * part_rows) % tok
            inside = (position >= start) & (position < stop)
            other = jnp.where(inside, 0.0, masked_score)
            rotary = []
            for part in range(parts):
                folded = material[part][block, part_rows:, :].astype(f32)
                pieces = width // part_rows
                flat = jnp.concatenate(
                    [folded[:, p * part_rows : (p + 1) * part_rows] for p in range(pieces)], axis=0
                )
                flat = jnp.concatenate([flat, flat], axis=0)
                rotary.append(flat.T)
            rotary = jnp.concatenate(rotary, axis=0)
            rows = slice(block * tok, (block + 1) * tok)
            side[0, rows, :] = jnp.where(low, rotary, other).astype(bf16)
            side[1, rows, :] = jnp.where(low, other, rotary).astype(bf16)

    def latents(block):
        return jnp.concatenate([m[block, :part_rows, :] for m in material], axis=0)

    held = {}

    def project(into, weight, pair, block):
        rows, columns = slice(block * tok, (block + 1) * tok), slice(pair * 256, (pair + 1) * 256)
        into[rows, columns] = jnp.dot(
            latents(block), weight[:, columns], preferred_element_type=f32
        ).astype(bf16)

    def score(head, block):
        rows = slice(block * tok, (block + 1) * tok)
        columns = slice(head * HEAD_DIM, (head + 1) * HEAD_DIM)
        pair, odd = divmod(head, 2)
        if block == 0:
            rotary = q_rope[:, pair * 128 : (pair + 1) * 128]
            held["query", head] = jnp.concatenate(
                [q_nope[:, columns], jnp.where(low != (odd == 1), rotary, query_side[...])], axis=1
            )
        key = jnp.concatenate([keys[rows, columns], side[odd, rows, :]], axis=1)
        scores = lax.dot_general(held["query", head], key, NT, preferred_element_type=f32)
        if first_back + block == 0:
            query_at = lax.broadcasted_iota(jnp.int32, (tok, tok), 0)
            key_at = lax.broadcasted_iota(jnp.int32, (tok, tok), 1)
            key_at = (key_at + place[1] * part_rows) % tok
            scores = jnp.where(key_at <= query_at, scores, masked_score)
        score_refs[head % 2][:, rows] = scores
        top = jnp.maximum(scores[:, :128], scores[:, 128:])
        held["top", head] = top if block == 0 else jnp.maximum(held["top", head], top)
        if block == blocks - 1:
            top = jnp.max(held["top", head], axis=1, keepdims=True) * scale
            if not first:
                earlier = stat_in[0, :, head : head + 1]
                top = jnp.maximum(top, earlier)
                held["fade", head] = jnp.exp2(earlier - top)
            held["top", head] = top

    def raise_(head, block):
        rows = slice(block * tok, (block + 1) * tok)
        raised = jnp.exp2(score_refs[head % 2][:, rows] * scale - held["top", head])
        weight_refs[head % 2][:, rows] = raised.astype(bf16)

    def mix(head):
        columns = slice(head * HEAD_DIM, (head + 1) * HEAD_DIM)
        value = jnp.concatenate([values[:, columns], jnp.ones((span, 128), bf16)], axis=1)
        mixed = jnp.dot(weight_refs[head % 2][...], value, preferred_element_type=f32)
        mixed, denom = mixed[:, :128], mixed[:, 128:]
        if not first:
            mixed = mixed + acc_in[:, columns] * held["fade", head]
            denom = denom + stat_in[0, :, GROUP + head : GROUP + head + 1] * held["fade", head]
        if last:
            out[:, columns] = (mixed / denom).astype(bf16)
        else:
            acc_out[:, columns] = mixed
            stat_out[0, :, head : head + 1] = held["top", head]
            stat_out[0, :, GROUP + head : GROUP + head + 1] = denom[:, :1]

    def together(*lists):
        for at in range(max(map(len, lists))):
            for each in lists:
                if at < len(each):
                    each[at]()

    def over(call, *args):
        return [functools.partial(call, *args, block) for block in range(blocks)]

    pairs = GROUP // 2
    together(over(project, keys, w_key, 0))
    together(over(score, 0))
    for pair in range(pairs):
        even, odd = 2 * pair, 2 * pair + 1
        together(over(project, values, w_value, pair), over(raise_, even))
        together(over(score, odd))
        mix(even)
        if pair + 1 < pairs:
            together(over(project, keys, w_key, pair + 1), over(raise_, odd))
            together(over(score, even + 2))
        else:
            together(over(raise_, odd))
        mix(odd)


def attend(lengths, place, material, q_nope, q_rope, w_key, w_value, state, first_back, last):
    tok, wide = q_nope.shape
    heads = wide // HEAD_DIM
    rope = q_rope.shape[1] // heads
    blocks, parts = material[0].shape[0], len(material)
    span, columns = blocks * tok, GROUP * HEAD_DIM
    whole = lambda x: pl.BlockSpec(x.shape, lambda g: (0,) * x.ndim)
    by_group = lambda rows, cols: pl.BlockSpec((rows, cols), lambda g: (0, g))
    stat = pl.BlockSpec((1, tok, 128), lambda g: (g, 0, 0))
    in_specs = [pl.BlockSpec(memory_space=pltpu.SMEM)] * 2
    in_specs += [whole(m) for m in material]
    in_specs += [by_group(tok, columns), by_group(tok, GROUP * rope)]
    in_specs += [by_group(w_key.shape[0], columns)] * 2
    if state:
        in_specs += [by_group(tok, columns), stat]
    if last:
        out_specs = by_group(tok, columns)
        out_shape = jax.ShapeDtypeStruct((tok, wide), bf16)
    else:
        out_specs = [by_group(tok, columns), stat]
        out_shape = [
            jax.ShapeDtypeStruct((tok, wide), f32),
            jax.ShapeDtypeStruct((heads // GROUP, tok, 128), f32),
        ]
    flops = 2 * span * heads * HEAD_DIM * (2 * w_key.shape[0] + 4 * tok)
    return pl.pallas_call(
        functools.partial(
            attend_kernel, (blocks, parts, first_back, not state, last, rope)
        ),
        grid=(heads // GROUP,),
        in_specs=in_specs,
        out_specs=out_specs,
        out_shape=out_shape,
        scratch_shapes=[
            pltpu.VMEM((span, columns), bf16),
            pltpu.VMEM((span, columns), bf16),
            pltpu.VMEM((2, span, 128), bf16),
            pltpu.VMEM((tok, 128), bf16),
            pltpu.VMEM((tok, span), f32),
            pltpu.VMEM((tok, span), f32),
            pltpu.VMEM((tok, span), bf16),
            pltpu.VMEM((tok, span), bf16),
        ],
        compiler_params=pltpu.CompilerParams(vmem_limit_bytes=40 << 20),
        cost_estimate=pl.CostEstimate(
            flops=flops, bytes_accessed=16 << 20, transcendentals=tok * span * heads
        ),
    )(lengths, place, *material, q_nope, q_rope, w_key, w_value, *state)


def shards(q_nope, q_rope, latents, rope_keys, doc_lengths, w_key, w_value):
    head_size = lax.axis_size("head")
    if head_size == 2:
        other_core = lambda x: [x, lax.ppermute(x, "head", [(0, 1), (1, 0)])]
        shift = lax.axis_index("head")
    else:
        latents = lax.all_gather(latents, "head", axis=0, tiled=True)
        rope_keys = lax.all_gather(rope_keys, "head", axis=1, tiled=True)
        other_core = lambda x: [x]
        shift = 0
    place = jnp.stack([lax.axis_index("ctx"), jnp.int32(shift)]).astype(jnp.int32)
    own = pack(latents, rope_keys)
    steps = (q_nope, q_rope, w_key, w_value)
    near = jnp.stack([from_behind(own, by) for by in (1, 2, 3)])
    far = from_behind(jnp.concatenate([own[None], near]), 4)
    state = attend(doc_lengths, place, other_core(own[None]), *steps, (), 0, False)
    state = attend(doc_lengths, place, other_core(near), *steps, state, 1, False)
    return attend(doc_lengths, place, other_core(far), *steps, state, 4, True)


def solution(mesh):
    return jax.shard_map(
        shards,
        mesh=mesh,
        in_specs=(
            P("ctx", "head"),
            P("ctx", "head"),
            P(("ctx", "head"), None),
            P(None, ("ctx", "head")),
            P(),
            P(None, "head"),
            P(None, "head"),
        ),
        out_specs=P("ctx", "head"),
        check_vma=False,
    )
```

time: 378 us -> 97.8 us (0.26); the launches traced: 371 us -> 96.1 us
  matrix products: 196 us -> 0 us
  Pallas kernels: 0 us -> 69.6 us
  other arithmetic: 70 us -> 1.12 us
  starting transfers between devices: 56.9 us -> 7.53 us
  local copies, waits for them, and re-layouts: 38.3 us -> 10.5 us
  blocking collectives: 6.08 us -> 0 us
  waiting for transfers between devices: 2.58 us -> 7.25 us
    dot_general x40 -> x0, matrix products: 196 us -> none  [the longest x8 68.1 us: shards(): jnp.einsum('qhr,rk->qhk', query_rope, rope_block, preferred_element_type=...]
    pallas_call x0 -> x4, Pallas kernels: none -> 69.6 us  [the longest x3 68 us: attend(): pl.pallas_call(functools.partial(attend_kernel, (blocks, parts, first_bac...]
    ppermute x14 -> x7, starting transfers between devices: 56.9 us -> 7.53 us  [the longest x4 6.96 us: from_behind(): lax.ppermute(x, 'ctx', [(i, (i + by) % length) for i in range(length)])]
    reshape x9 -> x0, local copies, waits for them, and re-layouts: 36.7 us -> none  [the longest x8 32.7 us: shards(): value_part = value_blocks[block].reshape(tok_rows, head_count, HEAD_DIM)]
    reduce_max x9 -> x0, other arithmetic: 34.1 us -> none  [shards(): row_top = jnp.max(all_scores, axis=2, keepdims=True)]
    reduce_sum x2 -> x0, other arithmetic: 33 us -> none  [the longest x1 32.9 us: shards(): denom_sum = jnp.sum(raised, axis=2)]
    unnamed x35 -> x18, local copies, waits for them, and re-layouts: 1.54 us -> 10.5 us
    all_gather x2 -> x0, blocking collectives: 6.08 us -> none  [the longest x1 3.96 us: shards(): lax.all_gather(latents, 'head', axis=0, tiled=True)]
  transfers between devices with their start and end apart: 14 -> 7, of which waited for: 2 -> 2; matrix products, arithmetic and copies ran while one was open for 53% -> 1% of each run, Pallas kernels for 0% -> 41%
where the time goes in v1:
time: 97.8 us; the launch traced here: 96.1 us
  Pallas kernels  69.6 us (71%)
  local copies, waits for them, and re-layouts  10.5 us (11%)
  starting transfers between devices  7.53 us (8%)
  waiting for transfers between devices  7.25 us (7%)
  other arithmetic  1.12 us (1%)
    pallas_call x3, Pallas kernels, attend(): pl.pallas_call(functools.partial(attend_kernel, (blocks, parts, first_bac...  68 us
    unnamed x18, local copies, waits for them, and re-layouts  10.5 us
    ppermute x4, waiting for transfers between devices, from_behind(): lax.ppermute(x, 'ctx', [(i, (i + by) % length) for i in range(length)])  7.24 us
    ppermute x4, starting transfers between devices, from_behind(): lax.ppermute(x, 'ctx', [(i, (i + by) % length) for i in range(length)])  6.96 us
  transfers between devices with their start and end apart: 7, of which 2 were waited for; matrix products, arithmetic and copies ran while one was open for 1% of the time, Pallas kernels for 41%

profile of v1, /device:TPU:0, one launch (start us, length us, event | category | flops | bytes accessed | tf_op | source)
XLA Modules:
  0.0 96.1 jit_solution(9741914560530439992)
XLA Ops:
  0.0 1.6 %shard_map.73 = bf16[144,512]{1,0:T(8,128)(2,1)} custom-call(bf16[128,512]{1,0:T(8,128)(2,1)} %latents.1, bf16[64,128]{1,0:T(8,128)(2,1)} %rope_keys.1), custom_call_target="tpu_custom_call" | custom-call | tf_op jit(solution)/shard_map/pallas_call | solution.py:40
  1.6 2.9 %collective-permute-start = (bf16[144,512]{1,0:T(8,128)(2,1)}, bf16[144,512]{1,0:T(8,128)(2,1)S(1)}, u32[]{:S(2)}, u32[]{:S(2)}) collective-permute-start(bf16[144,512]{1,0:T(8,128)(2,1)} %shard_map.73), channel_id=1, source_target_pairs={{0,2},{2,4},{4,6},{6,8},{8,10},{10,12},{12,14},{14,16},{16,18},{18... | collective-permute-start | bytes 442376 | tf_op jit(solution)/shard_map/ppermute | solution.py:22
  4.5 1.5 %collective-permute-start.1 = (bf16[144,512]{1,0:T(8,128)(2,1)}, bf16[144,512]{1,0:T(8,128)(2,1)S(1)}, u32[]{:S(2)}, u32[]{:S(2)}) collective-permute-start(bf16[144,512]{1,0:T(8,128)(2,1)} %shard_map.73), channel_id=1, source_target_pairs={{0,4},{2,6},{4,8},{6,10},{8,12},{10,14},{12,16},{14,18},{16,20},{1... | collective-permute-start | bytes 442376 | tf_op jit(solution)/shard_map/ppermute | solution.py:22
  6.0 2.4 %collective-permute-start.2 = (bf16[144,512]{1,0:T(8,128)(2,1)}, bf16[144,512]{1,0:T(8,128)(2,1)S(1)}, u32[]{:S(2)}, u32[]{:S(2)}) collective-permute-start(bf16[144,512]{1,0:T(8,128)(2,1)} %shard_map.73), channel_id=1, source_target_pairs={{0,6},{2,8},{4,10},{6,12},{8,14},{10,16},{12,18},{14,20},{16,22},{... | collective-permute-start | bytes 442376 | tf_op jit(solution)/shard_map/ppermute | solution.py:22
  8.5 0.0 collective-permute-start.6
  8.5 6.8 %collective-permute-done = bf16[144,512]{1,0:T(8,128)(2,1)S(1)} collective-permute-done((bf16[144,512]{1,0:T(8,128)(2,1)}, bf16[144,512]{1,0:T(8,128)(2,1)S(1)}, u32[]{:S(2)}, u32[]{:S(2)}) %collective-permute-start) | collective-permute-done | bytes 147488 | tf_op jit(solution)/shard_map/ppermute | solution.py:22
  15.3 0.4 collective-permute-done.1
  15.7 0.0 collective-permute-done.2
  15.7 1.0 %pad_maximum_fusion = bf16[4,144,512]{2,1,0:T(8,128)(2,1)S(1)} fusion(bf16[1,144,512]{2,1,0:T(8,128)(2,1)S(1)} %bitcast.13, bf16[1,144,512]{2,1,0:T(8,128)(2,1)S(1)} %bitcast.11, bf16[1,144,512]{2,1,0:T(8,128)(2,1)S(1)} %bitcast.9, bf16[1,144,512]{2,1,0:T(8,128)(2,1)} %bitcast.7), kind=kLoop, calls=%fused_computation | loop fusion | flops 884736 | bytes 1179648 | tf_op jit(solution)/shard_map/concatenate | solution.py:250
  16.7 0.1 collective-permute-start.3
  16.8 0.1 pad_maximum_fusion.1.refs_2_
  16.8 0.1 collective-permute-start.5
  16.9 0.1 pad_add_fusion.refs_1_
  17.0 0.0 collective-permute-done.6.refs_3_
  17.0 0.0 copy-start
  17.0 0.9 copy-done
  17.9 0.0 copy-start.1
  17.9 2.2 %copy-done.1 = bf16[512,4096]{1,0:T(8,128)(2,1)S(1)} copy-done((bf16[512,4096]{1,0:T(8,128)(2,1)S(1)}, bf16[512,4096]{1,0:T(8,128)(2,1)}, u32[]{:S(2)}) %copy-start.1) | copy-done | bytes 4194328
  20.1 0.0 copy-start.3
  20.1 1.6 %copy-done.3 = bf16[256,4096]{1,0:T(8,128)(2,1)S(1)} copy-done((bf16[256,4096]{1,0:T(8,128)(2,1)S(1)}, bf16[256,4096]{1,0:T(8,128)(2,1)}, u32[]{:S(2)}) %copy-start.3) | copy-done | bytes 2097176
  21.7 0.0 copy-start.4
  21.7 1.2 %copy-done.4 = bf16[256,2048]{1,0:T(8,128)(2,1)S(1)} copy-done((bf16[256,2048]{1,0:T(8,128)(2,1)S(1)}, bf16[256,2048]{1,0:T(8,128)(2,1)}, u32[]{:S(2)}) %copy-start.4) | copy-done | bytes 1048600
  22.9 0.0 copy-start.5
  22.9 0.7 copy-done.5
  23.6 0.0 copy-start.6
  23.6 14.1 %shard_map.74 = (f32[256,4096]{1,0:T(8,128)S(1)}, f32[8,256,128]{2,1,0:T(8,128)S(1)}) custom-call(s32[8]{0:T(128)S(1)} %copy-done.5, s32[2]{0:T(128)S(1)} %pad_add_fusion.refs_1_, bf16[1,144,512]{2,1,0:T(8,128)(2,1)S(1)} %bitcast.8, bf16[1,144,512]{2,1,0:T(8,128)(2,1)S(1)} %collective-permute-done.6.refs_3_, bf16[256,4096]{1,0:T(8,128)(2,1)S(1)} %copy-done.3, ...), custom_call_target="tpu_custom_call" | custom-call | flops 4294967296 | bytes 16777216 | tf_op jit(solution)/shard_map/pallas_call | solution.py:211
  37.7 0.0 copy-start.7
  37.7 2.0 %copy-done.7 = f32[256,4096]{1,0:T(8,128)} copy-done((f32[256,4096]{1,0:T(8,128)}, f32[256,4096]{1,0:T(8,128)S(1)}, u32[]{:S(2)}) %copy-start.7) | copy-done | bytes 4194328
  39.6 0.0 collective-permute-done.3.refs_2_
  39.6 0.5 collective-permute-start.4
  40.1 0.0 collective-permute-done.5.refs_3_
  40.1 0.0 copy-done.6
  40.1 0.0 copy-start.2
  40.1 25.7 %shard_map.75 = (f32[256,4096]{1,0:T(8,128)S(1)}, f32[8,256,128]{2,1,0:T(8,128)S(1)}) custom-call(s32[8]{0:T(128)S(1)} %copy-done.6, s32[2]{0:T(128)S(1)} %pad_add_fusion.refs_1_, bf16[3,144,512]{2,1,0:T(8,128)(2,1)S(1)} %pad_maximum_fusion.1.refs_2_, bf16[3,144,512]{2,1,0:T(8,128)(2,1)S(1)} %collective-permute-done.5.refs_3_, ...), custom_call_target="tpu_custom_call" | custom-call | flops 12884901888 | bytes 16777216 | tf_op jit(solution)/shard_map/pallas_call | solution.py:211
  65.8 0.0 copy-start.8
  65.8 2.0 %copy-done.8 = f32[256,4096]{1,0:T(8,128)} copy-done((f32[256,4096]{1,0:T(8,128)}, f32[256,4096]{1,0:T(8,128)S(1)}, u32[]{:S(2)}) %copy-start.8) | copy-done | bytes 4194328
  67.8 0.0 collective-permute-done.4.refs_3_
  67.8 0.0 copy-done.2
  67.8 28.3 %shard_map.76 = bf16[256,4096]{1,0:T(8,128)(2,1)} custom-call(s32[8]{0:T(128)S(1)} %copy-done.6, s32[2]{0:T(128)S(1)} %pad_add_fusion.refs_1_, bf16[4,144,512]{2,1,0:T(8,128)(2,1)S(1)} %collective-permute-done.3.refs_2_, bf16[4,144,512]{2,1,0:T(8,128)(2,1)S(1)} %collective-permute-done.4.refs_3_, bf16[256,4096]{1,0:T(8,128)(2,1)S(1)} %copy-done.3, ...), custom_call_target="tpu_custom_call" | custom-call | flops 17179869184 | bytes 16777216 | tf_op jit(solution)/shard_map/pallas_call | solution.py:211
Async XLA Ops:
  1.6 13.7 %collective-permute-start = (bf16[144,512]{1,0:T(8,128)(2,1)}, bf16[144,512]{1,0:T(8,128)(2,1)S(1)}, u32[]{:S(2)}, u32[]{:S(2)}) collective-permute-start(bf16[144,512]{1,0:T(8,128)(2,1)} %shard_map.73), channel_id=1, source_target_pairs={{0,2},{2,4},{4,6},{6,8},{8,10},{10,12},{12,14},{14,16},{16,18},{18... | collective-permute-start | bytes 442376 | tf_op jit(solution)/shard_map/ppermute | solution.py:22
  4.5 11.2 %collective-permute-start.1 = (bf16[144,512]{1,0:T(8,128)(2,1)}, bf16[144,512]{1,0:T(8,128)(2,1)S(1)}, u32[]{:S(2)}, u32[]{:S(2)}) collective-permute-start(bf16[144,512]{1,0:T(8,128)(2,1)} %shard_map.73), channel_id=1, source_target_pairs={{0,4},{2,6},{4,8},{6,10},{8,12},{10,14},{12,16},{14,18},{16,20},{1... | collective-permute-start | bytes 442376 | tf_op jit(solution)/shard_map/ppermute | solution.py:22
  6.0 9.7 %collective-permute-start.2 = (bf16[144,512]{1,0:T(8,128)(2,1)}, bf16[144,512]{1,0:T(8,128)(2,1)S(1)}, u32[]{:S(2)}, u32[]{:S(2)}) collective-permute-start(bf16[144,512]{1,0:T(8,128)(2,1)} %shard_map.73), channel_id=1, source_target_pairs={{0,6},{2,8},{4,10},{6,12},{8,14},{10,16},{12,18},{14,20},{16,22},{... | collective-permute-start | bytes 442376 | tf_op jit(solution)/shard_map/ppermute | solution.py:22
  8.5 8.5 %collective-permute-start.6 = (bf16[1,144,512]{2,1,0:T(8,128)(2,1)}, bf16[1,144,512]{2,1,0:T(8,128)(2,1)S(1)}, u32[]{:S(2)}, u32[]{:S(2)}) collective-permute-start(bf16[1,144,512]{2,1,0:T(8,128)(2,1)} %bitcast.6), channel_id=1, source_target_pairs={{0,1},{1,0},{2,3},{3,2},{4,5},{5,4},{6,7},{7,6},{8,9},{9,8},{10,11... | collective-permute-start | bytes 442376 | tf_op jit(solution)/shard_map/ppermute | solution.py:239
  16.7 22.9 %collective-permute-start.3 = (bf16[4,144,512]{2,1,0:T(8,128)(2,1)S(1)}, bf16[4,144,512]{2,1,0:T(8,128)(2,1)S(1)}, u32[]{:S(2)}, u32[]{:S(2)}) collective-permute-start(bf16[4,144,512]{2,1,0:T(8,128)(2,1)S(1)} %pad_maximum_fusion), channel_id=1, source_target_pairs={{0,8},{2,10},{4,12},{6,14},{8,16},{10,18},{12,20},{14,22},{16,24},... | collective-permute-start | bytes 1769480 | tf_op jit(solution)/shard_map/ppermute | solution.py:22
  16.8 23.3 %collective-permute-start.5 = (bf16[3,144,512]{2,1,0:T(8,128)(2,1)S(1)}, bf16[3,144,512]{2,1,0:T(8,128)(2,1)S(1)}, u32[]{:S(2)}, u32[]{:S(2)}) collective-permute-start(bf16[3,144,512]{2,1,0:T(8,128)(2,1)S(1)} %pad_maximum_fusion.1.refs_2_), channel_id=1, source_target_pairs={{0,1},{1,0},{2,3},{3,2},{4,5},{5,4},{6,7},{7,6},{8,9},{9,8},{10,11... | collective-permute-start | bytes 1327112 | tf_op jit(solution)/shard_map/ppermute | solution.py:239
  17.0 0.9 copy-start
  17.9 2.2 %copy-start.1 = (bf16[512,4096]{1,0:T(8,128)(2,1)S(1)}, bf16[512,4096]{1,0:T(8,128)(2,1)}, u32[]{:S(2)}) copy-start(bf16[512,4096]{1,0:T(8,128)(2,1)} %refs_6_.5) | copy-start | bytes 12582916
  20.1 1.6 %copy-start.3 = (bf16[256,4096]{1,0:T(8,128)(2,1)S(1)}, bf16[256,4096]{1,0:T(8,128)(2,1)}, u32[]{:S(2)}) copy-start(bf16[256,4096]{1,0:T(8,128)(2,1)} %refs_4_.5) | copy-start | bytes 6291460
  21.7 1.2 %copy-start.4 = (bf16[256,2048]{1,0:T(8,128)(2,1)S(1)}, bf16[256,2048]{1,0:T(8,128)(2,1)}, u32[]{:S(2)}) copy-start(bf16[256,2048]{1,0:T(8,128)(2,1)} %refs_5_.5) | copy-start | bytes 3145732
  22.9 0.7 copy-start.5
  23.6 16.5 %copy-start.6 = (s32[8]{0:T(128)S(1)}, s32[8]{0:T(128)}, u32[]{:S(2)}) copy-start(s32[8]{0:T(128)} %refs_0_.5) | copy-start | bytes 100
  37.7 2.0 %copy-start.7 = (f32[256,4096]{1,0:T(8,128)}, f32[256,4096]{1,0:T(8,128)S(1)}, u32[]{:S(2)}) copy-start(f32[256,4096]{1,0:T(8,128)S(1)} %get-tuple-element.9.refs_8_) | copy-start | bytes 12582916
  39.6 28.2 %collective-permute-start.4 = (bf16[4,144,512]{2,1,0:T(8,128)(2,1)S(1)}, bf16[4,144,512]{2,1,0:T(8,128)(2,1)S(1)}, u32[]{:S(2)}, u32[]{:S(2)}) collective-permute-start(bf16[4,144,512]{2,1,0:T(8,128)(2,1)S(1)} %collective-permute-done.3.refs_2_), channel_id=1, source_target_pairs={{0,1},{1,0},{2,3},{3,2},{4,5},{5,4},{6,7},{7,6},{8,9},{9,8},{10,11... | collective-permute-start | bytes 1769480 | tf_op jit(solution)/shard_map/ppermute | solution.py:239
  40.1 27.7 %copy-start.2 = (bf16[512,4096]{1,0:T(8,128)(2,1)S(1)}, bf16[512,4096]{1,0:T(8,128)(2,1)}, u32[]{:S(2)}) copy-start(bf16[512,4096]{1,0:T(8,128)(2,1)} %refs_7_.5) | copy-start | bytes 12582916
  65.8 2.0 %copy-start.8 = (f32[256,4096]{1,0:T(8,128)}, f32[256,4096]{1,0:T(8,128)S(1)}, u32[]{:S(2)}) copy-start(f32[256,4096]{1,0:T(8,128)S(1)} %get-tuple-element.11.refs_8_) | copy-start | bytes 12582916

commit v2 on v1

v2 whole, which is shorter than its diff:
```python
import functools
import math

import jax
import jax.numpy as jnp
from jax import lax
from jax.experimental import pallas as pl
from jax.experimental.pallas import tpu as pltpu
from jax.sharding import PartitionSpec as P

HEAD_DIM = 128
WINDOW = 8

masked_score = -1e30
f32, bf16 = jnp.float32, jnp.bfloat16
NT = (((1,), (1,)), ((), ()))


def from_behind(x, by):
    length = lax.axis_size("ctx")
    return lax.ppermute(x, "ctx", [(i, (i + by) % length) for i in range(length)])


def pack_kernel(latents, rope_keys, packed):
    rows = latents.shape[0]
    packed[:rows, :] = latents[...]
    lanes = rope_keys.shape[1]
    pieces = latents.shape[1] // lanes
    tall = rope_keys.shape[0] // pieces
    for piece in range(pieces):
        packed[rows:, piece * lanes : (piece + 1) * lanes] = rope_keys[
            piece * tall : (piece + 1) * tall, :
        ]


def pack(latents, rope_keys):
    rows, width = latents.shape
    below = rope_keys.size // width
    return pl.pallas_call(
        pack_kernel, out_shape=jax.ShapeDtypeStruct((rows + below, width), bf16)
    )(latents, rope_keys)


def weave(*lists):
    calls = [((at + 0.5) / len(each), turn, call) for turn, each in enumerate(lists) for at, call in enumerate(each)]
    for _, _, call in sorted(calls, key=lambda entry: entry[:2]):
        call()


def attend_kernel(shape, *refs):
    blocks, parts, first_back, first, last = shape
    lengths, place = refs[:2]
    material = refs[2 : 2 + parts]
    rest = list(refs[2 + parts :])
    take = lambda count: [rest.pop(0) for _ in range(count)]
    sources = take(4 if first else 6)
    targets = take(1 if last else 2)
    landed = take(len(sources))
    leaving = take(len(targets))
    keys, values, scores_of, weights_of, tops, fades, side, query_side, later, came, went = take(11)
    w_key, q_nope, q_rope, w_value = landed[:4]
    tok = q_nope.shape[1]
    groups = q_nope.shape[0]
    span = blocks * tok
    part_rows = tok // parts
    width = w_key.shape[1]
    rope = q_rope.shape[2] // 4
    scale = math.log2(math.e) / math.sqrt(HEAD_DIM + rope)
    lane = lax.broadcasted_iota(jnp.int32, (tok, 128), 1)
    low = lane < 64

    def columns_of(ref, group, wide):
        if len(ref.shape) == 3:
            return ref.at[group]
        start = group * wide
        return ref.at[:, pl.ds(start if isinstance(start, int) else pl.multiple_of(start, wide), wide)]

    def arrival(which, group):
        into = landed[which].at[group]
        return pltpu.make_async_copy(
            columns_of(sources[which], group, into.shape[-1]), into, came.at[which, group]
        )

    def departure(which, group):
        from_ = leaving[which].at[group]
        return pltpu.make_async_copy(
            from_, columns_of(targets[which], group, from_.shape[-1]), went.at[which, group]
        )

    for group in range(groups):
        for which in range(len(sources)):
            arrival(which, group).start()

    def depart(group):
        for which in range(len(targets)):
            departure(which, group).start()

    at = lax.broadcasted_iota(jnp.int32, (8, 128), 1) % 64
    start, stop = jnp.zeros((8, 128), jnp.int32), jnp.zeros((8, 128), jnp.int32)
    before = jnp.int32(0)
    for doc in range(lengths.shape[0]):
        after = before + lengths[doc]
        start = jnp.where(at == doc, before, start)
        stop = jnp.where(at == doc, after, stop)
        before = after
    start, stop = start[:1], stop[:1]
    row = lax.broadcasted_iota(jnp.int32, (tok, 128), 0)
    position = place[0] * tok + row
    inside = (position >= start) & (position < stop)
    query_side[...] = jnp.where(inside, 1.0, 0.0).astype(bf16)

    def turned(at):
        at = at + place[1] * part_rows
        return jnp.where(at >= tok, at - tok, at)

    if first_back == 0:
        query_at = lax.broadcasted_iota(jnp.int32, (tok, tok), 0)
        key_at = turned(lax.broadcasted_iota(jnp.int32, (tok, tok), 1))
        later[...] = jnp.where(key_at <= query_at, 0.0, masked_score)
    for block in range(blocks):
        position = (place[0] - first_back - block) * tok + turned(row)
        inside = (position >= start) & (position < stop)
        other = jnp.where(inside, 0.0, masked_score)
        rotary = []
        for part in range(parts):
            folded = material[part][block, part_rows:, :].astype(f32)
            pieces = width // part_rows
            flat = jnp.concatenate(
                [folded[:, p * part_rows : (p + 1) * part_rows] for p in range(pieces)], axis=0
            )
            flat = jnp.concatenate([flat, flat], axis=0)
            rotary.append(flat.T)
        rotary = jnp.concatenate(rotary, axis=0)
        rows = slice(block * tok, (block + 1) * tok)
        side[0, rows, :] = jnp.where(low, rotary, other).astype(bf16)
        side[1, rows, :] = jnp.where(low, other, rotary).astype(bf16)

    def latents(block):
        return jnp.concatenate([m[block, :part_rows, :] for m in material], axis=0)

    def project(into, weight, pair, block):
        group, half = pair
        rows = slice(block * tok, (block + 1) * tok)
        columns = slice(half * 256, (half + 1) * 256)
        into[half, rows, :] = jnp.dot(
            latents(block), weight[group, :, columns], preferred_element_type=f32
        ).astype(bf16)

    queries = {}

    def score(pair, odd, block):
        group, half = pair
        rows = slice(block * tok, (block + 1) * tok)
        columns = slice(odd * HEAD_DIM, (odd + 1) * HEAD_DIM)
        head = slice((2 * half + odd) * HEAD_DIM, (2 * half + odd + 1) * HEAD_DIM)
        if block == 0:
            rotary = q_rope[group, :, half * 128 : (half + 1) * 128]
            queries[0] = jnp.concatenate(
                [q_nope[group, :, head], jnp.where(low != (odd == 1), rotary, query_side[...])], axis=1
            )
        key = jnp.concatenate([keys[half, rows, columns], side[odd, rows, :]], axis=1)
        scores = lax.dot_general(queries[0], key, NT, preferred_element_type=f32)
        if first_back + block == 0:
            scores = scores + later[...]
        scores_of[half, odd, :, rows] = scores
        top = jnp.maximum(scores[:, :128], scores[:, 128:])
        queries["top"] = top if block == 0 else jnp.maximum(queries["top"], top)
        if block == blocks - 1:
            top = jnp.max(queries["top"], axis=1, keepdims=True) * scale
            if not first:
                lane_at = 4 * half + odd
                earlier = landed[5][group, :, lane_at : lane_at + 1]
                top = jnp.maximum(top, earlier)
                fades[half, odd] = jnp.broadcast_to(jnp.exp2(earlier - top), (tok, 128))
            tops[half, odd] = jnp.broadcast_to(top, (tok, 128))

    def raise_(pair, odd, block):
        group, half = pair
        rows = slice(block * tok, (block + 1) * tok)
        top = jnp.concatenate([tops[half, odd]] * (tok // 128), axis=1)
        raised = jnp.exp2(scores_of[half, odd, :, rows] * scale - top)
        weights_of[half, odd, :, rows] = raised.astype(bf16)

    def mix(pair, odd):
        group, half = pair
        columns = slice(odd * HEAD_DIM, (odd + 1) * HEAD_DIM)
        head = slice((2 * half + odd) * HEAD_DIM, (2 * half + odd + 1) * HEAD_DIM)
        value = jnp.concatenate([values[half, :, columns], jnp.ones((span, 128), bf16)], axis=1)
        mixed = jnp.dot(weights_of[half, odd], value, preferred_element_type=f32)
        mixed, denom = mixed[:, :128], mixed[:, 128:]
        if not first:
            fade = fades[half, odd]
            mixed = mixed + landed[4][group, :, head] * fade
            lane_at = 4 * half + 2 + odd
            denom = denom + landed[5][group, :, lane_at : lane_at + 1] * fade
        if last:
            mixed = mixed / denom
        else:
            stat = leaving[1][group]
            stat = jnp.where(lane == 4 * half + odd, tops[half, odd], stat)
            leaving[1][group] = jnp.where(lane == 4 * half + 2 + odd, denom, stat)
        leaving[0][group, :, head] = mixed.astype(leaving[0].dtype)

    def each_block(call, *args):
        return [functools.partial(call, *args, block) for block in range(blocks)]

    def both_heads(call, pair):
        return each_block(call, pair, 0) + each_block(call, pair, 1)

    def turn(mixed, scored, keyed):
        raises = both_heads(raise_, mixed)
        half = len(raises) // 2 if keyed else len(raises)
        if scored:
            weave(both_heads(score, scored), raises[:half])
        else:
            weave(raises[:half])
        if keyed:
            weave(each_block(project, keys, w_key, keyed), raises[half:])
        mix(mixed, 0)
        mix(mixed, 1)
        if scored:
            weave(each_block(project, values, w_value, scored))

    arrival(0, 0).wait()
    weave(each_block(project, keys, w_key, (0, 0)))
    for which in range(1, len(sources)):
        arrival(which, 0).wait()
    weave(both_heads(score, (0, 0)), each_block(project, keys, w_key, (0, 1)))
    weave(each_block(project, values, w_value, (0, 0)))

    def two_turns(group, carry):
        for which in range(len(sources)):
            arrival(which, group + 1).wait()

        @pl.when(group > 0)
        def _():
            depart(group - 1)

        turn((group, 0), (group, 1), (group + 1, 0))
        turn((group, 1), (group + 1, 0), (group + 1, 1))
        return carry

    lax.fori_loop(0, groups - 1, two_turns, 0)
    if groups > 1:
        depart(groups - 2)
    turn((groups - 1, 0), (groups - 1, 1), None)
    turn((groups - 1, 1), None, None)
    depart(groups - 1)
    for group in range(groups):
        for which in range(len(targets)):
            departure(which, group).wait()


def attend(lengths, place, material, q_nope, q_rope, w_key, w_value, state, first_back, last):
    tok, wide = q_nope.shape
    groups = wide // HEAD_DIM // 4
    width = w_key.shape[0]
    blocks, parts = material[0].shape[0], len(material)
    span = blocks * tok
    any_ = pl.BlockSpec(memory_space=pl.ANY)
    sources = [w_key, q_nope, q_rope, w_value, *state]
    if last:
        out_shape = [jax.ShapeDtypeStruct((tok, wide), bf16)]
    else:
        out_shape = [
            jax.ShapeDtypeStruct((tok, wide), f32),
            jax.ShapeDtypeStruct((groups, tok, 128), f32),
        ]
    by_pair = lambda x: pltpu.VMEM(
        (groups, x.shape[-2], x.shape[-1] // (groups if len(x.shape) == 2 else 1)), x.dtype
    )
    flops = 2 * span * wide * (2 * width + 4 * tok)
    return pl.pallas_call(
        functools.partial(attend_kernel, (blocks, parts, first_back, not state, last)),
        in_specs=[pl.BlockSpec(memory_space=pltpu.SMEM)] * 2
        + [pl.BlockSpec(memory_space=pltpu.VMEM)] * parts
        + [any_] * len(sources),
        out_specs=[any_] * len(out_shape),
        out_shape=out_shape,
        scratch_shapes=[by_pair(x) for x in sources + out_shape]
        + [
            pltpu.VMEM((2, span, 256), bf16),
            pltpu.VMEM((2, span, 256), bf16),
            pltpu.VMEM((2, 2, tok, span), f32),
            pltpu.VMEM((2, 2, tok, span), bf16),
            pltpu.VMEM((2, 2, tok, 128), f32),
            pltpu.VMEM((2, 2, tok, 128), f32),
            pltpu.VMEM((2, span, 128), bf16),
            pltpu.VMEM((tok, 128), bf16),
            pltpu.VMEM((tok, tok), f32),
            pltpu.SemaphoreType.DMA((len(sources), groups)),
            pltpu.SemaphoreType.DMA((len(out_shape), groups)),
        ],
        compiler_params=pltpu.CompilerParams(vmem_limit_bytes=60 << 20),
        cost_estimate=pl.CostEstimate(
            flops=flops, bytes_accessed=16 << 20, transcendentals=tok * span * wide // HEAD_DIM
        ),
    )(lengths, place, *material, *sources)


def shards(q_nope, q_rope, latents, rope_keys, doc_lengths, w_key, w_value):
    head_size = lax.axis_size("head")
    if head_size == 2:
        other_core = lambda x: [x, lax.ppermute(x, "head", [(0, 1), (1, 0)])]
        shift = lax.axis_index("head")
    else:
        latents = lax.all_gather(latents, "head", axis=0, tiled=True)
        rope_keys = lax.all_gather(rope_keys, "head", axis=1, tiled=True)
        other_core = lambda x: [x]
        shift = 0
    place = jnp.stack([lax.axis_index("ctx"), jnp.int32(shift)]).astype(jnp.int32)
    own = pack(latents, rope_keys)
    steps = (q_nope, q_rope, w_key, w_value)
    near = jnp.stack([from_behind(own, by) for by in (1, 2, 3)])
    far = from_behind(jnp.concatenate([own[None], near]), 4)
    state = attend(doc_lengths, place, other_core(own[None]), *steps, (), 0, False)
    state = attend(doc_lengths, place, other_core(near), *steps, state, 1, False)
    return attend(doc_lengths, place, other_core(far), *steps, state, 4, True)[0]


def solution(mesh):
    return jax.shard_map(
        shards,
        mesh=mesh,
        in_specs=(
            P("ctx", "head"),
            P("ctx", "head"),
            P(("ctx", "head"), None),
            P(None, ("ctx", "head")),
            P(),
            P(None, "head"),
            P(None, "head"),
        ),
        out_specs=P("ctx", "head"),
        check_vma=False,
    )
```

time: 97.8 us -> 81.7 us (0.84)
  the two profiles are of different devices: /device:TPU:0 before, /device:TPU:5 now
where the time goes in v2:
time: 81.7 us; the launch traced here: 81.4 us
  Pallas kernels  56.9 us (70%)
  waiting for transfers between devices  10.7 us (13%)
  starting transfers between devices  9.86 us (12%)
  local copies, waits for them, and re-layouts  2.27 us (3%)
  other arithmetic  1.65 us (2%)
    pallas_call x3, Pallas kernels, attend(): pl.pallas_call(functools.partial(attend_kernel, (blocks, parts, first_bac...  55.4 us
    ppermute x4, waiting for transfers between devices, from_behind(): lax.ppermute(x, 'ctx', [(i, (i + by) % length) for i in range(length)])  10.6 us
    ppermute x3, starting transfers between devices, shards(): other_core = lambda x: [x, lax.ppermute(x, 'head', [(0, 1), (1, 0)])]  5.19 us
    ppermute x4, starting transfers between devices, from_behind(): lax.ppermute(x, 'ctx', [(i, (i + by) % length) for i in range(length)])  4.68 us
    unnamed x10, local copies, waits for them, and re-layouts  2.27 us
  transfers between devices with their start and end apart: 7, of which 3 were waited for; matrix products, arithmetic and copies ran while one was open for 2% of the time, Pallas kernels for 37%

profile of v2, /device:TPU:5, one launch (start us, length us, event | category | flops | bytes accessed | tf_op | source)
XLA Modules:
  0.0 81.4 jit_solution(6479198180060542741)
XLA Ops:
  0.0 1.6 %shard_map.73 = bf16[144,512]{1,0:T(8,128)(2,1)} custom-call(bf16[128,512]{1,0:T(8,128)(2,1)} %latents.1, bf16[64,128]{1,0:T(8,128)(2,1)} %rope_keys.1), custom_call_target="tpu_custom_call" | custom-call | tf_op jit(solution)/shard_map/pallas_call | solution.py:39
  1.6 1.2 %collective-permute-start = (bf16[144,512]{1,0:T(8,128)(2,1)}, bf16[144,512]{1,0:T(8,128)(2,1)S(1)}, u32[]{:S(2)}, u32[]{:S(2)}) collective-permute-start(bf16[144,512]{1,0:T(8,128)(2,1)} %shard_map.73), channel_id=1, source_target_pairs={{0,2},{2,4},{4,6},{6,8},{8,10},{10,12},{12,14},{14,16},{16,18},{18... | collective-permute-start | bytes 442376 | tf_op jit(solution)/shard_map/ppermute | solution.py:21
  2.8 1.2 %collective-permute-start.1 = (bf16[144,512]{1,0:T(8,128)(2,1)}, bf16[144,512]{1,0:T(8,128)(2,1)S(1)}, u32[]{:S(2)}, u32[]{:S(2)}) collective-permute-start(bf16[144,512]{1,0:T(8,128)(2,1)} %shard_map.73), channel_id=1, source_target_pairs={{0,4},{2,6},{4,8},{6,10},{8,12},{10,14},{12,16},{14,18},{16,20},{1... | collective-permute-start | bytes 442376 | tf_op jit(solution)/shard_map/ppermute | solution.py:21
  4.0 2.2 %collective-permute-start.2 = (bf16[144,512]{1,0:T(8,128)(2,1)}, bf16[144,512]{1,0:T(8,128)(2,1)S(1)}, u32[]{:S(2)}, u32[]{:S(2)}) collective-permute-start(bf16[144,512]{1,0:T(8,128)(2,1)} %shard_map.73), channel_id=1, source_target_pairs={{0,6},{2,8},{4,10},{6,12},{8,14},{10,16},{12,18},{14,20},{16,22},{... | collective-permute-start | bytes 442376 | tf_op jit(solution)/shard_map/ppermute | solution.py:21
  6.2 1.5 %collective-permute-start.6 = (bf16[1,144,512]{2,1,0:T(8,128)(2,1)}, bf16[1,144,512]{2,1,0:T(8,128)(2,1)S(1)}, u32[]{:S(2)}, u32[]{:S(2)}) collective-permute-start(bf16[1,144,512]{2,1,0:T(8,128)(2,1)} %bitcast.12), channel_id=1, source_target_pairs={{0,1},{1,0},{2,3},{3,2},{4,5},{5,4},{6,7},{7,6},{8,9},{9,8},{10,11... | collective-permute-start | bytes 442376 | tf_op jit(solution)/shard_map/ppermute | solution.py:304
  7.7 0.0 collective-permute-done
  7.7 3.9 %collective-permute-done.1 = bf16[144,512]{1,0:T(8,128)(2,1)S(1)} collective-permute-done((bf16[144,512]{1,0:T(8,128)(2,1)}, bf16[144,512]{1,0:T(8,128)(2,1)S(1)}, u32[]{:S(2)}, u32[]{:S(2)}) %collective-permute-start.1) | collective-permute-done | bytes 147488 | tf_op jit(solution)/shard_map/ppermute | solution.py:21
  11.6 4.5 %collective-permute-done.2 = bf16[144,512]{1,0:T(8,128)(2,1)S(1)} collective-permute-done((bf16[144,512]{1,0:T(8,128)(2,1)}, bf16[144,512]{1,0:T(8,128)(2,1)S(1)}, u32[]{:S(2)}, u32[]{:S(2)}) %collective-permute-start.2) | collective-permute-done | bytes 147488 | tf_op jit(solution)/shard_map/ppermute | solution.py:21
  16.1 1.0 %pad_maximum_fusion = bf16[4,144,512]{2,1,0:T(8,128)(2,1)S(1)} fusion(bf16[1,144,512]{2,1,0:T(8,128)(2,1)S(1)} %bitcast.10, bf16[1,144,512]{2,1,0:T(8,128)(2,1)S(1)} %bitcast.8, bf16[1,144,512]{2,1,0:T(8,128)(2,1)S(1)} %bitcast.6, bf16[1,144,512]{2,1,0:T(8,128)(2,1)} %bitcast.13), kind=kLoop, calls=%fused_computation | loop fusion | flops 884736 | bytes 1179648 | tf_op jit(solution)/shard_map/concatenate | solution.py:315
  17.1 0.1 collective-permute-start.3
  17.2 0.1 pad_maximum_fusion.1.refs_2_
  17.2 0.0 copy-start
  17.2 1.4 %collective-permute-start.5 = (bf16[3,144,512]{2,1,0:T(8,128)(2,1)S(1)}, bf16[3,144,512]{2,1,0:T(8,128)(2,1)S(1)}, u32[]{:S(2)}, u32[]{:S(2)}) collective-permute-start(bf16[3,144,512]{2,1,0:T(8,128)(2,1)S(1)} %pad_maximum_fusion.1.refs_2_), channel_id=1, source_target_pairs={{0,1},{1,0},{2,3},{3,2},{4,5},{5,4},{6,7},{7,6},{8,9},{9,8},{10,11... | collective-permute-start | bytes 1327112 | tf_op jit(solution)/shard_map/ppermute | solution.py:304
  18.6 0.6 pad_add_fusion.refs_1_
  19.2 0.0 collective-permute-done.6.refs_3_
  19.2 0.0 copy-start.4
  19.2 0.7 copy-done.4
  19.9 10.2 %shard_map.74 = (f32[256,4096]{1,0:T(8,128)}, f32[8,256,128]{2,1,0:T(8,128)}) custom-call(s32[8]{0:T(128)} %refs_0_.5, s32[2]{0:T(128)} %pad_add_fusion.refs_1_, bf16[1,144,512]{2,1,0:T(8,128)(2,1)} %bitcast.14, bf16[1,144,512]{2,1,0:T(8,128)(2,1)} %copy-done.4, bf16[512,4096]{1,0:T(8,128)(2,1)} %refs_4_.5, bf16[256,4096]{1,0:T(8,128)(2,1)} %refs_5_.5, ...), custom_call_target="tpu_custom_call" | custom-call | flops 4294967296 | bytes 16777216 | tf_op jit(solution)/shard_map/pallas_call | solution.py:273
  30.1 0.0 copy-done
  30.2 2.3 %collective-permute-done.3.refs_2_ = bf16[4,144,512]{2,1,0:T(8,128)(2,1)S(1)} collective-permute-done((bf16[4,144,512]{2,1,0:T(8,128)(2,1)S(1)}, bf16[4,144,512]{2,1,0:T(8,128)(2,1)S(1)}, u32[]{:S(2)}, u32[]{:S(2)}) %collective-permute-start.3) | collective-permute-done | bytes 589856 | tf_op jit(solution)/shard_map/ppermute | solution.py:21
  32.4 0.0 copy-start.1
  32.4 2.3 %collective-permute-start.4 = (bf16[4,144,512]{2,1,0:T(8,128)(2,1)S(1)}, bf16[4,144,512]{2,1,0:T(8,128)(2,1)S(1)}, u32[]{:S(2)}, u32[]{:S(2)}) collective-permute-start(bf16[4,144,512]{2,1,0:T(8,128)(2,1)S(1)} %collective-permute-done.3.refs_2_), channel_id=1, source_target_pairs={{0,1},{1,0},{2,3},{3,2},{4,5},{5,4},{6,7},{7,6},{8,9},{9,8},{10,11... | collective-permute-start | bytes 1769480 | tf_op jit(solution)/shard_map/ppermute | solution.py:304
  34.7 0.0 collective-permute-done.5.refs_3_
  34.7 0.0 copy-start.3
  34.7 0.8 copy-done.3
  35.5 19.7 %shard_map.75 = (f32[256,4096]{1,0:T(8,128)}, f32[8,256,128]{2,1,0:T(8,128)}) custom-call(s32[8]{0:T(128)} %refs_0_.5, s32[2]{0:T(128)} %pad_add_fusion.refs_1_, bf16[3,144,512]{2,1,0:T(8,128)(2,1)} %copy-done, bf16[3,144,512]{2,1,0:T(8,128)(2,1)} %copy-done.3, bf16[512,4096]{1,0:T(8,128)(2,1)} %refs_4_.5, bf16[256,4096]{1,0:T(8,128)(2,1)} %refs_5_.5, ...), custom_call_target="tpu_custom_call" | custom-call | flops 12884901888 | bytes 16777216 | tf_op jit(solution)/shard_map/pallas_call | solution.py:273
  55.2 0.0 copy-done.1
  55.2 0.0 collective-permute-done.4.refs_3_
  55.2 0.0 copy-start.2
  55.2 0.8 copy-done.2
  56.0 25.4 %shard_map.76 = bf16[256,4096]{1,0:T(8,128)(2,1)} custom-call(s32[8]{0:T(128)} %refs_0_.5, s32[2]{0:T(128)} %pad_add_fusion.refs_1_, bf16[4,144,512]{2,1,0:T(8,128)(2,1)} %copy-done.1, bf16[4,144,512]{2,1,0:T(8,128)(2,1)} %copy-done.2, bf16[512,4096]{1,0:T(8,128)(2,1)} %refs_4_.5, bf16[256,4096]{1,0:T(8,128)(2,1)} %refs_5_.5, bf16[256,2048]{1,0:T(8,128)(2,1)} %refs_6_.5, ...), custom_call_target="tpu_custom_call" | custom-call | flops 17179869184 | bytes 16777216 | tf_op jit(solution)/shard_map/pallas_call | solution.py:273
Async XLA Ops:
  1.6 6.1 %collective-permute-start = (bf16[144,512]{1,0:T(8,128)(2,1)}, bf16[144,512]{1,0:T(8,128)(2,1)S(1)}, u32[]{:S(2)}, u32[]{:S(2)}) collective-permute-start(bf16[144,512]{1,0:T(8,128)(2,1)} %shard_map.73), channel_id=1, source_target_pairs={{0,2},{2,4},{4,6},{6,8},{8,10},{10,12},{12,14},{14,16},{16,18},{18... | collective-permute-start | bytes 442376 | tf_op jit(solution)/shard_map/ppermute | solution.py:21
  2.8 8.8 %collective-permute-start.1 = (bf16[144,512]{1,0:T(8,128)(2,1)}, bf16[144,512]{1,0:T(8,128)(2,1)S(1)}, u32[]{:S(2)}, u32[]{:S(2)}) collective-permute-start(bf16[144,512]{1,0:T(8,128)(2,1)} %shard_map.73), channel_id=1, source_target_pairs={{0,4},{2,6},{4,8},{6,10},{8,12},{10,14},{12,16},{14,18},{16,20},{1... | collective-permute-start | bytes 442376 | tf_op jit(solution)/shard_map/ppermute | solution.py:21
  4.0 12.1 %collective-permute-start.2 = (bf16[144,512]{1,0:T(8,128)(2,1)}, bf16[144,512]{1,0:T(8,128)(2,1)S(1)}, u32[]{:S(2)}, u32[]{:S(2)}) collective-permute-start(bf16[144,512]{1,0:T(8,128)(2,1)} %shard_map.73), channel_id=1, source_target_pairs={{0,6},{2,8},{4,10},{6,12},{8,14},{10,16},{12,18},{14,20},{16,22},{... | collective-permute-start | bytes 442376 | tf_op jit(solution)/shard_map/ppermute | solution.py:21
  6.2 13.0 %collective-permute-start.6 = (bf16[1,144,512]{2,1,0:T(8,128)(2,1)}, bf16[1,144,512]{2,1,0:T(8,128)(2,1)S(1)}, u32[]{:S(2)}, u32[]{:S(2)}) collective-permute-start(bf16[1,144,512]{2,1,0:T(8,128)(2,1)} %bitcast.12), channel_id=1, source_target_pairs={{0,1},{1,0},{2,3},{3,2},{4,5},{5,4},{6,7},{7,6},{8,9},{9,8},{10,11... | collective-permute-start | bytes 442376 | tf_op jit(solution)/shard_map/ppermute | solution.py:304
  17.1 15.3 %collective-permute-start.3 = (bf16[4,144,512]{2,1,0:T(8,128)(2,1)S(1)}, bf16[4,144,512]{2,1,0:T(8,128)(2,1)S(1)}, u32[]{:S(2)}, u32[]{:S(2)}) collective-permute-start(bf16[4,144,512]{2,1,0:T(8,128)(2,1)S(1)} %pad_maximum_fusion), channel_id=1, source_target_pairs={{0,8},{2,10},{4,12},{6,14},{8,16},{10,18},{12,20},{14,22},{16,24},... | collective-permute-start | bytes 1769480 | tf_op jit(solution)/shard_map/ppermute | solution.py:21
  17.2 12.9 %copy-start = (bf16[3,144,512]{2,1,0:T(8,128)(2,1)}, bf16[3,144,512]{2,1,0:T(8,128)(2,1)S(1)}, u32[]{:S(2)}) copy-start(bf16[3,144,512]{2,1,0:T(8,128)(2,1)S(1)} %pad_maximum_fusion.1.refs_2_) | copy-start | bytes 1327108
  17.2 17.5 %collective-permute-start.5 = (bf16[3,144,512]{2,1,0:T(8,128)(2,1)S(1)}, bf16[3,144,512]{2,1,0:T(8,128)(2,1)S(1)}, u32[]{:S(2)}, u32[]{:S(2)}) collective-permute-start(bf16[3,144,512]{2,1,0:T(8,128)(2,1)S(1)} %pad_maximum_fusion.1.refs_2_), channel_id=1, source_target_pairs={{0,1},{1,0},{2,3},{3,2},{4,5},{5,4},{6,7},{7,6},{8,9},{9,8},{10,11... | collective-permute-start | bytes 1327112 | tf_op jit(solution)/shard_map/ppermute | solution.py:304
  19.2 0.7 copy-start.4
  32.4 22.7 %copy-start.1 = (bf16[4,144,512]{2,1,0:T(8,128)(2,1)}, bf16[4,144,512]{2,1,0:T(8,128)(2,1)S(1)}, u32[]{:S(2)}) copy-start(bf16[4,144,512]{2,1,0:T(8,128)(2,1)S(1)} %collective-permute-done.3.refs_2_) | copy-start | bytes 1769476
  32.4 22.8 %collective-permute-start.4 = (bf16[4,144,512]{2,1,0:T(8,128)(2,1)S(1)}, bf16[4,144,512]{2,1,0:T(8,128)(2,1)S(1)}, u32[]{:S(2)}, u32[]{:S(2)}) collective-permute-start(bf16[4,144,512]{2,1,0:T(8,128)(2,1)S(1)} %collective-permute-done.3.refs_2_), channel_id=1, source_target_pairs={{0,1},{1,0},{2,3},{3,2},{4,5},{5,4},{6,7},{7,6},{8,9},{9,8},{10,11... | collective-permute-start | bytes 1769480 | tf_op jit(solution)/shard_map/ppermute | solution.py:304
  34.7 0.8 copy-start.3
  55.2 0.8 %copy-start.2 = (bf16[4,144,512]{2,1,0:T(8,128)(2,1)}, bf16[4,144,512]{2,1,0:T(8,128)(2,1)S(1)}, u32[]{:S(2)}) copy-start(bf16[4,144,512]{2,1,0:T(8,128)(2,1)S(1)} %collective-permute-done.4.refs_3_) | copy-start | bytes 1769476

commit v3 on v2

--- a/solution.py
+++ b/solution.py
@@ -48,21 +48,24 @@
 
 
 def attend_kernel(shape, *refs):
-    blocks, parts, first_back, first, last = shape
+    pieces, arrays, diagonal, first, last = shape
     lengths, place = refs[:2]
-    material = refs[2 : 2 + parts]
-    rest = list(refs[2 + parts :])
+    rest = list(refs[2:])
     take = lambda count: [rest.pop(0) for _ in range(count)]
+    packed = take(arrays)
     sources = take(4 if first else 6)
     targets = take(1 if last else 2)
+    material = take(arrays)
     landed = take(len(sources))
     leaving = take(len(targets))
-    keys, values, scores_of, weights_of, tops, fades, side, query_side, later, came, went = take(11)
+    keys, values, scores_of, weights_of, tops, fades, side, query_side, later, unpacked, came, went = take(12)
     w_key, q_nope, q_rope, w_value = landed[:4]
     tok = q_nope.shape[1]
     groups = q_nope.shape[0]
-    span = blocks * tok
-    part_rows = tok // parts
+    part_rows = part_rows_of(packed[0].shape, w_key.shape[1], q_rope.shape[2] // 4)
+    span = len(pieces) * part_rows
+    bounds = [(at, min(at + tok, span)) for at in range(0, span, tok)]
+    blocks = len(bounds)
     width = w_key.shape[1]
     rope = q_rope.shape[2] // 4
     scale = math.log2(math.e) / math.sqrt(HEAD_DIM + rope)
@@ -87,9 +90,17 @@
             from_, columns_of(targets[which], group, from_.shape[-1]), went.at[which, group]
         )
 
+    arrivals = [
+        pltpu.make_async_copy(from_, into, unpacked.at[at])
+        for at, (from_, into) in enumerate(zip(packed, material))
+    ]
+    arrival(0, 0).start()
+    for each in arrivals:
+        each.start()
     for group in range(groups):
         for which in range(len(sources)):
-            arrival(which, group).start()
+            if (which, group) != (0, 0):
+                arrival(which, group).start()
 
     def depart(group):
         for which in range(len(targets)):
@@ -113,34 +124,39 @@
         at = at + place[1] * part_rows
         return jnp.where(at >= tok, at - tok, at)
 
-    if first_back == 0:
+    if diagonal:
         query_at = lax.broadcasted_iota(jnp.int32, (tok, tok), 0)
         key_at = turned(lax.broadcasted_iota(jnp.int32, (tok, tok), 1))
         later[...] = jnp.where(key_at <= query_at, 0.0, masked_score)
-    for block in range(blocks):
-        position = (place[0] - first_back - block) * tok + turned(row)
+    for each in arrivals:
+        each.wait()
+    folds = width // part_rows
+    row = lax.broadcasted_iota(jnp.int32, (part_rows, 128), 0)
+    low_rows = lax.broadcasted_iota(jnp.int32, (part_rows, 128), 1) < 64
+    for at, (array, index, distance, other) in enumerate(pieces):
+        part = 1 - place[1] if other else place[1]
+        position = (place[0] - distance) * tok + part * part_rows + row
         inside = (position >= start) & (position < stop)
-        other = jnp.where(inside, 0.0, masked_score)
-        rotary = []
-        for part in range(parts):
-            folded = material[part][block, part_rows:, :].astype(f32)
-            pieces = width // part_rows
-            flat = jnp.concatenate(
-                [folded[:, p * part_rows : (p + 1) * part_rows] for p in range(pieces)], axis=0
-            )
-            flat = jnp.concatenate([flat, flat], axis=0)
-            rotary.append(flat.T)
-        rotary = jnp.concatenate(rotary, axis=0)
-        rows = slice(block * tok, (block + 1) * tok)
-        side[0, rows, :] = jnp.where(low, rotary, other).astype(bf16)
-        side[1, rows, :] = jnp.where(low, other, rotary).astype(bf16)
+        elsewhere = jnp.where(inside, 0.0, masked_score)
+        folded = material[array][index, part_rows:, :].astype(f32)
+        flat = jnp.concatenate(
+            [folded[:, p * part_rows : (p + 1) * part_rows] for p in range(folds)] * 2, axis=0
+        )
+        rotary = flat.T
+        rows = slice(at * part_rows, (at + 1) * part_rows)
+        side[0, rows, :] = jnp.where(low_rows, rotary, elsewhere).astype(bf16)
+        side[1, rows, :] = jnp.where(low_rows, elsewhere, rotary).astype(bf16)
 
     def latents(block):
-        return jnp.concatenate([m[block, :part_rows, :] for m in material], axis=0)
+        low_end, high_end = (bound // part_rows for bound in bounds[block])
+        return jnp.concatenate(
+            [material[array][index, :part_rows, :] for array, index, _, _ in pieces[low_end:high_end]],
+            axis=0,
+        )
 
     def project(into, weight, pair, block):
         group, half = pair
-        rows = slice(block * tok, (block + 1) * tok)
+        rows = slice(*bounds[block])
         columns = slice(half * 256, (half + 1) * 256)
         into[half, rows, :] = jnp.dot(
             latents(block), weight[group, :, columns], preferred_element_type=f32
@@ -150,7 +166,7 @@
 
     def score(pair, odd, block):
         group, half = pair
-        rows = slice(block * tok, (block + 1) * tok)
+        rows = slice(*bounds[block])
         columns = slice(odd * HEAD_DIM, (odd + 1) * HEAD_DIM)
         head = slice((2 * half + odd) * HEAD_DIM, (2 * half + odd + 1) * HEAD_DIM)
         if block == 0:
@@ -160,10 +176,12 @@
             )
         key = jnp.concatenate([keys[half, rows, columns], side[odd, rows, :]], axis=1)
         scores = lax.dot_general(queries[0], key, NT, preferred_element_type=f32)
-        if first_back + block == 0:
+        if diagonal and block == 0:
             scores = scores + later[...]
         scores_of[half, odd, :, rows] = scores
-        top = jnp.maximum(scores[:, :128], scores[:, 128:])
+        top = functools.reduce(
+            jnp.maximum, [scores[:, at : at + 128] for at in range(0, scores.shape[1], 128)]
+        )
         queries["top"] = top if block == 0 else jnp.maximum(queries["top"], top)
         if block == blocks - 1:
             top = jnp.max(queries["top"], axis=1, keepdims=True) * scale
@@ -176,8 +194,8 @@
 
     def raise_(pair, odd, block):
         group, half = pair
-        rows = slice(block * tok, (block + 1) * tok)
-        top = jnp.concatenate([tops[half, odd]] * (tok // 128), axis=1)
+        rows = slice(*bounds[block])
+        top = jnp.concatenate([tops[half, odd]] * ((rows.stop - rows.start) // 128), axis=1)
         raised = jnp.exp2(scores_of[half, odd, :, rows] * scale - top)
         weights_of[half, odd, :, rows] = raised.astype(bf16)
 
@@ -251,12 +269,16 @@
             departure(which, group).wait()
 
 
-def attend(lengths, place, material, q_nope, q_rope, w_key, w_value, state, first_back, last):
+def part_rows_of(packed_shape, width, rope):
+    return packed_shape[1] * width // (width + rope)
+
+
+def attend(lengths, place, material, pieces, q_nope, q_rope, w_key, w_value, state, diagonal, last):
     tok, wide = q_nope.shape
     groups = wide // HEAD_DIM // 4
     width = w_key.shape[0]
-    blocks, parts = material[0].shape[0], len(material)
-    span = blocks * tok
+    rope = q_rope.shape[1] * HEAD_DIM // wide
+    span = len(pieces) * part_rows_of(material[0].shape, width, rope)
     any_ = pl.BlockSpec(memory_space=pl.ANY)
     sources = [w_key, q_nope, q_rope, w_value, *state]
     if last:
@@ -266,18 +288,18 @@
             jax.ShapeDtypeStruct((tok, wide), f32),
             jax.ShapeDtypeStruct((groups, tok, 128), f32),
         ]
-    by_pair = lambda x: pltpu.VMEM(
+    by_group = lambda x: pltpu.VMEM(
         (groups, x.shape[-2], x.shape[-1] // (groups if len(x.shape) == 2 else 1)), x.dtype
     )
     flops = 2 * span * wide * (2 * width + 4 * tok)
     return pl.pallas_call(
-        functools.partial(attend_kernel, (blocks, parts, first_back, not state, last)),
+        functools.partial(attend_kernel, (pieces, len(material), diagonal, not state, last)),
         in_specs=[pl.BlockSpec(memory_space=pltpu.SMEM)] * 2
-        + [pl.BlockSpec(memory_space=pltpu.VMEM)] * parts
-        + [any_] * len(sources),
+        + [any_] * (len(material) + len(sources)),
         out_specs=[any_] * len(out_shape),
         out_shape=out_shape,
-        scratch_shapes=[by_pair(x) for x in sources + out_shape]
+        scratch_shapes=[pltpu.VMEM(x.shape, x.dtype) for x in material]
+        + [by_group(x) for x in sources + out_shape]
         + [
             pltpu.VMEM((2, span, 256), bf16),
             pltpu.VMEM((2, span, 256), bf16),
@@ -288,6 +310,7 @@
             pltpu.VMEM((2, span, 128), bf16),
             pltpu.VMEM((tok, 128), bf16),
             pltpu.VMEM((tok, tok), f32),
+            pltpu.SemaphoreType.DMA((len(material),)),
             pltpu.SemaphoreType.DMA((len(sources), groups)),
             pltpu.SemaphoreType.DMA((len(out_shape), groups)),
         ],
@@ -299,23 +322,36 @@
 
 
 def shards(q_nope, q_rope, latents, rope_keys, doc_lengths, w_key, w_value):
-    head_size = lax.axis_size("head")
-    if head_size == 2:
-        other_core = lambda x: [x, lax.ppermute(x, "head", [(0, 1), (1, 0)])]
-        shift = lax.axis_index("head")
+    halves = lax.axis_size("head") == 2
+    place = [lax.axis_index("ctx"), lax.axis_index("head") if halves else jnp.int32(0)]
+    place = jnp.stack(place).astype(jnp.int32)
+    if halves:
+        swap = lambda x: lax.ppermute(x, "head", [(0, 1), (1, 0)])
     else:
         latents = lax.all_gather(latents, "head", axis=0, tiled=True)
         rope_keys = lax.all_gather(rope_keys, "head", axis=1, tiled=True)
-        other_core = lambda x: [x]
-        shift = 0
-    place = jnp.stack([lax.axis_index("ctx"), jnp.int32(shift)]).astype(jnp.int32)
+    run = lambda material, pieces, state, last: attend(
+        doc_lengths, place, material, pieces, q_nope, q_rope, w_key, w_value, state, not state, last
+    )
     own = pack(latents, rope_keys)
-    steps = (q_nope, q_rope, w_key, w_value)
-    near = jnp.stack([from_behind(own, by) for by in (1, 2, 3)])
+    near = [from_behind(own, by) for by in (1, 2, 3)]
+    if halves:
+        state = run([own[None], swap(own[None])], [(0, 0, 0, False), (1, 0, 0, True)], (), False)
+    else:
+        state = run([own[None]], [(0, 0, 0, False)], (), False)
+    near, state = lax.optimization_barrier((near, state))
+    near = jnp.stack(near)
     far = from_behind(jnp.concatenate([own[None], near]), 4)
-    state = attend(doc_lengths, place, other_core(own[None]), *steps, (), 0, False)
-    state = attend(doc_lengths, place, other_core(near), *steps, state, 1, False)
-    return attend(doc_lengths, place, other_core(far), *steps, state, 4, True)[0]
+    near_pieces = [(0, block - 1, block, False) for block in (1, 2, 3)]
+    far_pieces = [(0, block - 4, block, False) for block in (4, 5, 6, 7)]
+    if halves:
+        other_near = swap(near)
+        state = run([near], near_pieces, state, False)
+        far_pieces += [(1, block - 4, block, True) for block in (4, 5, 6, 7)]
+        far_pieces += [(2, block - 1, block, True) for block in (1, 2, 3)]
+        return run([far, swap(far), other_near], far_pieces, state, True)[0]
+    state = run([near], near_pieces, state, False)
+    return run([far], far_pieces, state, True)[0]
 
 
 def solution(mesh):

time: 81.7 us -> 101 us (1.24)
  the two profiles are of different devices: /device:TPU:5 before, /device:TPU:0 now
where the time goes in v3:
time: 101 us; the launch traced here: 100 us
  Pallas kernels  75 us (74%)
  waiting for transfers between devices  15 us (15%)
  starting transfers between devices  7.89 us (8%)
  local copies, waits for them, and re-layouts  1.61 us (2%)
    pallas_call x3, Pallas kernels, attend(): pl.pallas_call(functools.partial(attend_kernel, (pieces, len(material), d...  73.4 us
    ppermute x4, waiting for transfers between devices, from_behind(): lax.ppermute(x, 'ctx', [(i, (i + by) % length) for i in range(length)])  15 us
    ppermute x4, starting transfers between devices, from_behind(): lax.ppermute(x, 'ctx', [(i, (i + by) % length) for i in range(length)])  7.37 us
  transfers between devices with their start and end apart: 7, of which 1 were waited for; matrix products, arithmetic and copies ran while one was open for 1% of the time, Pallas kernels for 34%

profile of v3, /device:TPU:0, one launch (start us, length us, event | category | flops | bytes accessed | tf_op | source)
XLA Modules:
  0.0 100.5 jit_solution(7413470685224005713)
XLA Ops:
  0.0 1.6 %shard_map.73 = bf16[144,512]{1,0:T(8,128)(2,1)} custom-call(bf16[128,512]{1,0:T(8,128)(2,1)} %latents.1, bf16[64,128]{1,0:T(8,128)(2,1)} %rope_keys.1), custom_call_target="tpu_custom_call" | custom-call | tf_op jit(solution)/shard_map/pallas_call | solution.py:39
  1.6 0.5 collective-permute-start.3
  2.0 3.4 %collective-permute-start.2 = (bf16[144,512]{1,0:T(8,128)(2,1)}, bf16[144,512]{1,0:T(8,128)(2,1)S(1)}, u32[]{:S(2)}, u32[]{:S(2)}) collective-permute-start(bf16[144,512]{1,0:T(8,128)(2,1)} %shard_map.73), channel_id=1, source_target_pairs={{0,6},{2,8},{4,10},{6,12},{8,14},{10,16},{12,18},{14,20},{16,22},{... | collective-permute-start | bytes 442376 | tf_op jit(solution)/shard_map/ppermute | solution.py:21
  5.5 1.5 %collective-permute-start.1 = (bf16[144,512]{1,0:T(8,128)(2,1)}, bf16[144,512]{1,0:T(8,128)(2,1)S(1)}, u32[]{:S(2)}, u32[]{:S(2)}) collective-permute-start(bf16[144,512]{1,0:T(8,128)(2,1)} %shard_map.73), channel_id=1, source_target_pairs={{0,4},{2,6},{4,8},{6,10},{8,12},{10,14},{12,16},{14,18},{16,20},{1... | collective-permute-start | bytes 442376 | tf_op jit(solution)/shard_map/ppermute | solution.py:21
  7.0 0.6 collective-permute-start
  7.6 0.6 pad_add_fusion.refs_1_
  8.2 0.0 copy-start
  8.2 0.0 collective-permute-done.3.refs_3_
  8.2 0.0 copy-start.5
  8.2 0.6 copy-done.5
  8.8 13.1 %shard_map.74 = (f32[256,4096]{1,0:T(8,128)}, f32[8,256,128]{2,1,0:T(8,128)}) custom-call(s32[8]{0:T(128)} %refs_0_.5, s32[2]{0:T(128)} %pad_add_fusion.refs_1_, bf16[1,144,512]{2,1,0:T(8,128)(2,1)} %bitcast.13, bf16[1,144,512]{2,1,0:T(8,128)(2,1)} %copy-done.5, bf16[512,4096]{1,0:T(8,128)(2,1)} %refs_5_.5, bf16[256,4096]{1,0:T(8,128)(2,1)} %refs_6_.5, ...), custom_call_target="tpu_custom_call" | custom-call | flops 4294967296 | bytes 16777216 | tf_op jit(solution)/shard_map/pallas_call | solution.py:295
  22.0 0.0 collective-permute-done.2
  22.0 0.0 collective-permute-done.1
  22.0 0.0 collective-permute-done
  22.0 0.0 copy-done
  22.0 0.1 pad_maximum_fusion
  22.1 1.8 %collective-permute-start.4 = (bf16[4,144,512]{2,1,0:T(8,128)(2,1)S(1)}, bf16[4,144,512]{2,1,0:T(8,128)(2,1)S(1)}, u32[]{:S(2)}, u32[]{:S(2)}) collective-permute-start(bf16[4,144,512]{2,1,0:T(8,128)(2,1)S(1)} %pad_maximum_fusion), channel_id=1, source_target_pairs={{0,8},{2,10},{4,12},{6,14},{8,16},{10,18},{12,20},{14,22},{16,24},... | collective-permute-start | bytes 1769480 | tf_op jit(solution)/shard_map/ppermute | solution.py:21
  23.9 0.1 pad_maximum_fusion.1.refs_2_
  24.0 0.0 copy-start.1
  24.0 0.1 collective-permute-start.6
  24.1 15.0 %collective-permute-done.4.refs_2_ = bf16[4,144,512]{2,1,0:T(8,128)(2,1)S(1)} collective-permute-done((bf16[4,144,512]{2,1,0:T(8,128)(2,1)S(1)}, bf16[4,144,512]{2,1,0:T(8,128)(2,1)S(1)}, u32[]{:S(2)}, u32[]{:S(2)}) %collective-permute-start.4) | collective-permute-done | bytes 589856 | tf_op jit(solution)/shard_map/ppermute | solution.py:21
  39.0 0.0 copy-start.2
  39.0 0.0 collective-permute-start.5
  39.0 0.0 copy-done.1
  39.0 20.9 %shard_map.75 = (f32[256,4096]{1,0:T(8,128)}, f32[8,256,128]{2,1,0:T(8,128)}) custom-call(s32[8]{0:T(128)} %refs_0_.5, s32[2]{0:T(128)} %pad_add_fusion.refs_1_, bf16[3,144,512]{2,1,0:T(8,128)(2,1)} %copy-done.1, bf16[512,4096]{1,0:T(8,128)(2,1)} %refs_5_.5, bf16[256,4096]{1,0:T(8,128)(2,1)} %refs_6_.5, bf16[256,2048]{1,0:T(8,128)(2,1)} %refs_7_.3, ...), custom_call_target="tpu_custom_call" | custom-call | flops 6442450944 | bytes 16777216 | tf_op jit(solution)/shard_map/pallas_call | solution.py:295
  60.0 0.0 copy-done.2
  60.0 0.0 collective-permute-done.6.refs_4_
  60.0 0.0 copy-start.4
  60.0 0.0 collective-permute-done.5.refs_3_
  60.0 0.0 copy-start.3
  60.0 0.7 copy-done.4
  60.8 0.2 copy-done.3
  61.0 39.4 %shard_map.76 = bf16[256,4096]{1,0:T(8,128)(2,1)} custom-call(s32[8]{0:T(128)} %refs_0_.5, s32[2]{0:T(128)} %pad_add_fusion.refs_1_, bf16[4,144,512]{2,1,0:T(8,128)(2,1)} %copy-done.2, bf16[4,144,512]{2,1,0:T(8,128)(2,1)} %copy-done.3, bf16[3,144,512]{2,1,0:T(8,128)(2,1)} %copy-done.4, bf16[512,4096]{1,0:T(8,128)(2,1)} %refs_5_.5, ...), custom_call_target="tpu_custom_call" | custom-call | flops 23622320128 | bytes 16777216 | tf_op jit(solution)/shard_map/pallas_call | solution.py:295
Async XLA Ops:
  1.6 6.6 %collective-permute-start.3 = (bf16[1,144,512]{2,1,0:T(8,128)(2,1)}, bf16[1,144,512]{2,1,0:T(8,128)(2,1)S(1)}, u32[]{:S(2)}, u32[]{:S(2)}) collective-permute-start(bf16[1,144,512]{2,1,0:T(8,128)(2,1)} %bitcast.12), channel_id=1, source_target_pairs={{0,1},{1,0},{2,3},{3,2},{4,5},{5,4},{6,7},{7,6},{8,9},{9,8},{10,11... | collective-permute-start | bytes 442376 | tf_op jit(solution)/shard_map/ppermute | solution.py:329
  2.0 19.9 %collective-permute-start.2 = (bf16[144,512]{1,0:T(8,128)(2,1)}, bf16[144,512]{1,0:T(8,128)(2,1)S(1)}, u32[]{:S(2)}, u32[]{:S(2)}) collective-permute-start(bf16[144,512]{1,0:T(8,128)(2,1)} %shard_map.73), channel_id=1, source_target_pairs={{0,6},{2,8},{4,10},{6,12},{8,14},{10,16},{12,18},{14,20},{16,22},{... | collective-permute-start | bytes 442376 | tf_op jit(solution)/shard_map/ppermute | solution.py:21
  5.5 16.5 %collective-permute-start.1 = (bf16[144,512]{1,0:T(8,128)(2,1)}, bf16[144,512]{1,0:T(8,128)(2,1)S(1)}, u32[]{:S(2)}, u32[]{:S(2)}) collective-permute-start(bf16[144,512]{1,0:T(8,128)(2,1)} %shard_map.73), channel_id=1, source_target_pairs={{0,4},{2,6},{4,8},{6,10},{8,12},{10,14},{12,16},{14,18},{16,20},{1... | collective-permute-start | bytes 442376 | tf_op jit(solution)/shard_map/ppermute | solution.py:21
  7.0 15.0 %collective-permute-start = (bf16[144,512]{1,0:T(8,128)(2,1)}, bf16[144,512]{1,0:T(8,128)(2,1)S(1)}, u32[]{:S(2)}, u32[]{:S(2)}) collective-permute-start(bf16[144,512]{1,0:T(8,128)(2,1)} %shard_map.73), channel_id=1, source_target_pairs={{0,2},{2,4},{4,6},{6,8},{8,10},{10,12},{12,14},{14,16},{16,18},{18... | collective-permute-start | bytes 442376 | tf_op jit(solution)/shard_map/ppermute | solution.py:21
  8.2 13.8 %copy-start = (bf16[144,512]{1,0:T(8,128)(2,1)S(1)}, bf16[144,512]{1,0:T(8,128)(2,1)}, u32[]{:S(2)}) copy-start(bf16[144,512]{1,0:T(8,128)(2,1)} %shard_map.73) | copy-start | bytes 442372
  8.2 0.7 copy-start.5
  22.1 16.9 %collective-permute-start.4 = (bf16[4,144,512]{2,1,0:T(8,128)(2,1)S(1)}, bf16[4,144,512]{2,1,0:T(8,128)(2,1)S(1)}, u32[]{:S(2)}, u32[]{:S(2)}) collective-permute-start(bf16[4,144,512]{2,1,0:T(8,128)(2,1)S(1)} %pad_maximum_fusion), channel_id=1, source_target_pairs={{0,8},{2,10},{4,12},{6,14},{8,16},{10,18},{12,20},{14,22},{16,24},... | collective-permute-start | bytes 1769480 | tf_op jit(solution)/shard_map/ppermute | solution.py:21
  24.0 15.1 %copy-start.1 = (bf16[3,144,512]{2,1,0:T(8,128)(2,1)}, bf16[3,144,512]{2,1,0:T(8,128)(2,1)S(1)}, u32[]{:S(2)}) copy-start(bf16[3,144,512]{2,1,0:T(8,128)(2,1)S(1)} %pad_maximum_fusion.1.refs_2_) | copy-start | bytes 1327108
  24.0 36.0 %collective-permute-start.6 = (bf16[3,144,512]{2,1,0:T(8,128)(2,1)S(1)}, bf16[3,144,512]{2,1,0:T(8,128)(2,1)S(1)}, u32[]{:S(2)}, u32[]{:S(2)}) collective-permute-start(bf16[3,144,512]{2,1,0:T(8,128)(2,1)S(1)} %pad_maximum_fusion.1.refs_2_), channel_id=1, source_target_pairs={{0,1},{1,0},{2,3},{3,2},{4,5},{5,4},{6,7},{7,6},{8,9},{9,8},{10,11... | collective-permute-start | bytes 1327112 | tf_op jit(solution)/shard_map/ppermute | solution.py:329
  39.0 20.9 %copy-start.2 = (bf16[4,144,512]{2,1,0:T(8,128)(2,1)}, bf16[4,144,512]{2,1,0:T(8,128)(2,1)S(1)}, u32[]{:S(2)}) copy-start(bf16[4,144,512]{2,1,0:T(8,128)(2,1)S(1)} %collective-permute-done.4.refs_2_) | copy-start | bytes 1769476
  39.0 21.0 %collective-permute-start.5 = (bf16[4,144,512]{2,1,0:T(8,128)(2,1)S(1)}, bf16[4,144,512]{2,1,0:T(8,128)(2,1)S(1)}, u32[]{:S(2)}, u32[]{:S(2)}) collective-permute-start(bf16[4,144,512]{2,1,0:T(8,128)(2,1)S(1)} %collective-permute-done.4.refs_2_), channel_id=1, source_target_pairs={{0,1},{1,0},{2,3},{3,2},{4,5},{5,4},{6,7},{7,6},{8,9},{9,8},{10,11... | collective-permute-start | bytes 1769480 | tf_op jit(solution)/shard_map/ppermute | solution.py:329
  60.0 0.8 copy-start.4
  60.0 0.9 copy-start.3

commit v4 on v3

--- a/solution.py
+++ b/solution.py
@@ -55,7 +55,7 @@
     packed = take(arrays)
     sources = take(4 if first else 6)
     targets = take(1 if last else 2)
-    material = take(arrays)
+    material = packed
     landed = take(len(sources))
     leaving = take(len(targets))
     keys, values, scores_of, weights_of, tops, fades, side, query_side, later, unpacked, came, went = take(12)
@@ -90,17 +90,11 @@
             from_, columns_of(targets[which], group, from_.shape[-1]), went.at[which, group]
         )
 
-    arrivals = [
-        pltpu.make_async_copy(from_, into, unpacked.at[at])
-        for at, (from_, into) in enumerate(zip(packed, material))
-    ]
-    arrival(0, 0).start()
-    for each in arrivals:
-        each.start()
-    for group in range(groups):
+    for which in range(len(sources)):
+        arrival(which, 0).start()
+    for group in range(1, groups):
         for which in range(len(sources)):
-            if (which, group) != (0, 0):
-                arrival(which, group).start()
+            arrival(which, group).start()
 
     def depart(group):
         for which in range(len(targets)):
@@ -128,8 +122,6 @@
         query_at = lax.broadcasted_iota(jnp.int32, (tok, tok), 0)
         key_at = turned(lax.broadcasted_iota(jnp.int32, (tok, tok), 1))
         later[...] = jnp.where(key_at <= query_at, 0.0, masked_score)
-    for each in arrivals:
-        each.wait()
     folds = width // part_rows
     row = lax.broadcasted_iota(jnp.int32, (part_rows, 128), 0)
     low_rows = lax.broadcasted_iota(jnp.int32, (part_rows, 128), 1) < 64
@@ -295,11 +287,10 @@
     return pl.pallas_call(
         functools.partial(attend_kernel, (pieces, len(material), diagonal, not state, last)),
         in_specs=[pl.BlockSpec(memory_space=pltpu.SMEM)] * 2
-        + [any_] * (len(material) + len(sources)),
+        + [pl.BlockSpec(memory_space=pltpu.VMEM)] * len(material) + [any_] * len(sources),
         out_specs=[any_] * len(out_shape),
         out_shape=out_shape,
-        scratch_shapes=[pltpu.VMEM(x.shape, x.dtype) for x in material]
-        + [by_group(x) for x in sources + out_shape]
+        scratch_shapes=[by_group(x) for x in sources + out_shape]
         + [
             pltpu.VMEM((2, span, 256), bf16),
             pltpu.VMEM((2, span, 256), bf16),
@@ -345,13 +336,14 @@
     near_pieces = [(0, block - 1, block, False) for block in (1, 2, 3)]
     far_pieces = [(0, block - 4, block, False) for block in (4, 5, 6, 7)]
     if halves:
-        other_near = swap(near)
-        state = run([near], near_pieces, state, False)
+        near_pieces += [(1, block - 1, block, True) for block in (1, 2, 3)]
         far_pieces += [(1, block - 4, block, True) for block in (4, 5, 6, 7)]
-        far_pieces += [(2, block - 1, block, True) for block in (1, 2, 3)]
-        return run([far, swap(far), other_near], far_pieces, state, True)[0]
-    state = run([near], near_pieces, state, False)
-    return run([far], far_pieces, state, True)[0]
+        both = lambda x: [x, swap(x)]
+    else:
+        both = lambda x: [x]
+    state = run(both(near), near_pieces, state, False)
+    far, state = lax.optimization_barrier((far, state))
+    return run(both(far), far_pieces, state, True)[0]
 
 
 def solution(mesh):

time: 101 us -> 71.5 us (0.71)
  Pallas kernels: 75 us -> 57 us
  waiting for transfers between devices: 15 us -> 4.35 us
  starting transfers between devices: 7.89 us -> 6.8 us
    pallas_call x3, Pallas kernels: 73.4 us -> 55.4 us  [attend(): pl.pallas_call(functools.partial(attend_kernel, (pieces, len(material), d...]
    ppermute x4, waiting for transfers between devices: 15 us -> 1.32 us  [from_behind(): lax.ppermute(x, 'ctx', [(i, (i + by) % length) for i in range(length)])]
    ppermute x3, waiting for transfers between devices: 0.01 us -> 3.03 us  [shards(): swap = lambda x: lax.ppermute(x, 'head', [(0, 1), (1, 0)])]
    ppermute x4, starting transfers between devices: 7.37 us -> 6.07 us  [from_behind(): lax.ppermute(x, 'ctx', [(i, (i + by) % length) for i in range(length)])]
  transfers between devices with their start and end apart: 7 -> 7, of which waited for: 1 -> 3; matrix products, arithmetic and copies ran while one was open for 1% -> 1% of each run, Pallas kernels for 34% -> 42%
where the time goes in v4:
time: 71.5 us; the launch traced here: 71.3 us
  Pallas kernels  57 us (80%)
  starting transfers between devices  6.8 us (10%)
  waiting for transfers between devices  4.35 us (6%)
  local copies, waits for them, and re-layouts  2.24 us (3%)
    pallas_call x3, Pallas kernels, attend(): pl.pallas_call(functools.partial(attend_kernel, (pieces, len(material), d...  55.4 us
    ppermute x4, starting transfers between devices, from_behind(): lax.ppermute(x, 'ctx', [(i, (i + by) % length) for i in range(length)])  6.07 us
    ppermute x3, waiting for transfers between devices, shards(): swap = lambda x: lax.ppermute(x, 'head', [(0, 1), (1, 0)])  3.03 us
    unnamed x12, local copies, waits for them, and re-layouts  2.24 us
    pallas_call x1, Pallas kernels, pack(): pl.pallas_call(pack_kernel, out_shape=jax.ShapeDtypeStruct((rows + below,...  1.59 us
  transfers between devices with their start and end apart: 7, of which 3 were waited for; matrix products, arithmetic and copies ran while one was open for 1% of the time, Pallas kernels for 42%

profile of v4, /device:TPU:0, one launch (start us, length us, event | category | flops | bytes accessed | tf_op | source)
XLA Modules:
  0.0 71.3 jit_solution(14770593369371152346)
XLA Ops:
  0.0 1.6 %shard_map.73 = bf16[144,512]{1,0:T(8,128)(2,1)} custom-call(bf16[128,512]{1,0:T(8,128)(2,1)} %latents.1, bf16[64,128]{1,0:T(8,128)(2,1)} %rope_keys.1), custom_call_target="tpu_custom_call" | custom-call | tf_op jit(solution)/shard_map/pallas_call | solution.py:39
  1.6 0.5 collective-permute-start.3
  2.0 3.4 %collective-permute-start.2 = (bf16[144,512]{1,0:T(8,128)(2,1)}, bf16[144,512]{1,0:T(8,128)(2,1)S(1)}, u32[]{:S(2)}, u32[]{:S(2)}) collective-permute-start(bf16[144,512]{1,0:T(8,128)(2,1)} %shard_map.73), channel_id=1, source_target_pairs={{0,6},{2,8},{4,10},{6,12},{8,14},{10,16},{12,18},{14,20},{16,22},{... | collective-permute-start | bytes 442376 | tf_op jit(solution)/shard_map/ppermute | solution.py:21
  5.5 1.5 %collective-permute-start.1 = (bf16[144,512]{1,0:T(8,128)(2,1)}, bf16[144,512]{1,0:T(8,128)(2,1)S(1)}, u32[]{:S(2)}, u32[]{:S(2)}) collective-permute-start(bf16[144,512]{1,0:T(8,128)(2,1)} %shard_map.73), channel_id=1, source_target_pairs={{0,4},{2,6},{4,8},{6,10},{8,12},{10,14},{12,16},{14,18},{16,20},{1... | collective-permute-start | bytes 442376 | tf_op jit(solution)/shard_map/ppermute | solution.py:21
  7.0 0.6 collective-permute-start
  7.6 0.6 pad_add_fusion.refs_1_
  8.2 0.0 copy-start
  8.2 0.0 collective-permute-done.3.refs_3_
  8.2 0.0 copy-start.5
  8.2 0.7 copy-done.5
  8.8 10.2 %shard_map.74 = (f32[256,4096]{1,0:T(8,128)}, f32[8,256,128]{2,1,0:T(8,128)}) custom-call(s32[8]{0:T(128)} %refs_0_.5, s32[2]{0:T(128)} %pad_add_fusion.refs_1_, bf16[1,144,512]{2,1,0:T(8,128)(2,1)} %bitcast.13, bf16[1,144,512]{2,1,0:T(8,128)(2,1)} %copy-done.5, bf16[512,4096]{1,0:T(8,128)(2,1)} %refs_4_.5, bf16[256,4096]{1,0:T(8,128)(2,1)} %refs_5_.5, ...), custom_call_target="tpu_custom_call" | custom-call | flops 4294967296 | bytes 16777216 | tf_op jit(solution)/shard_map/pallas_call | solution.py:287
  19.1 0.0 collective-permute-done.2
  19.1 0.0 collective-permute-done.1
  19.1 1.3 %collective-permute-done = bf16[144,512]{1,0:T(8,128)(2,1)S(1)} collective-permute-done((bf16[144,512]{1,0:T(8,128)(2,1)}, bf16[144,512]{1,0:T(8,128)(2,1)S(1)}, u32[]{:S(2)}, u32[]{:S(2)}) %collective-permute-start) | collective-permute-done | bytes 147488 | tf_op jit(solution)/shard_map/ppermute | solution.py:21
  20.4 0.1 pad_maximum_fusion.1.refs_2_
  20.5 0.0 copy-start.1
  20.5 0.1 collective-permute-start.5
  20.5 0.0 copy-done
  20.5 0.1 pad_maximum_fusion
  20.6 0.5 collective-permute-start.4
  21.2 1.2 %collective-permute-done.5.refs_3_ = bf16[3,144,512]{2,1,0:T(8,128)(2,1)S(1)} collective-permute-done((bf16[3,144,512]{2,1,0:T(8,128)(2,1)S(1)}, bf16[3,144,512]{2,1,0:T(8,128)(2,1)S(1)}, u32[]{:S(2)}, u32[]{:S(2)}) %collective-permute-start.5) | collective-permute-done | bytes 442400 | tf_op jit(solution)/shard_map/ppermute | solution.py:320
  22.3 0.0 copy-done.1
  22.3 0.0 copy-start.4
  22.3 0.7 %copy-done.4 = bf16[3,144,512]{2,1,0:T(8,128)(2,1)} copy-done((bf16[3,144,512]{2,1,0:T(8,128)(2,1)}, bf16[3,144,512]{2,1,0:T(8,128)(2,1)S(1)}, u32[]{:S(2)}) %copy-start.4) | copy-done | bytes 442392
  23.1 19.7 %shard_map.75 = (f32[256,4096]{1,0:T(8,128)}, f32[8,256,128]{2,1,0:T(8,128)}) custom-call(s32[8]{0:T(128)} %refs_0_.5, s32[2]{0:T(128)} %pad_add_fusion.refs_1_, bf16[3,144,512]{2,1,0:T(8,128)(2,1)} %copy-done.1, bf16[3,144,512]{2,1,0:T(8,128)(2,1)} %copy-done.4, bf16[512,4096]{1,0:T(8,128)(2,1)} %refs_4_.5, bf16[256,4096]{1,0:T(8,128)(2,1)} %refs_5_.5, ...), custom_call_target="tpu_custom_call" | custom-call | flops 12884901888 | bytes 16777216 | tf_op jit(solution)/shard_map/pallas_call | solution.py:287
  42.8 0.0 collective-permute-done.4.refs_2_
  42.8 0.0 copy-start.2
  42.8 0.2 collective-permute-start.6
  43.0 1.9 %collective-permute-done.6.refs_3_ = bf16[4,144,512]{2,1,0:T(8,128)(2,1)S(1)} collective-permute-done((bf16[4,144,512]{2,1,0:T(8,128)(2,1)S(1)}, bf16[4,144,512]{2,1,0:T(8,128)(2,1)S(1)}, u32[]{:S(2)}, u32[]{:S(2)}) %collective-permute-start.6) | collective-permute-done | bytes 589856 | tf_op jit(solution)/shard_map/ppermute | solution.py:320
  44.9 0.0 copy-done.2
  44.9 0.0 copy-start.3
  44.9 0.8 %copy-done.3 = bf16[4,144,512]{2,1,0:T(8,128)(2,1)} copy-done((bf16[4,144,512]{2,1,0:T(8,128)(2,1)}, bf16[4,144,512]{2,1,0:T(8,128)(2,1)S(1)}, u32[]{:S(2)}) %copy-start.3) | copy-done | bytes 589848
  45.7 25.5 %shard_map.76 = bf16[256,4096]{1,0:T(8,128)(2,1)} custom-call(s32[8]{0:T(128)} %refs_0_.5, s32[2]{0:T(128)} %pad_add_fusion.refs_1_, bf16[4,144,512]{2,1,0:T(8,128)(2,1)} %copy-done.2, bf16[4,144,512]{2,1,0:T(8,128)(2,1)} %copy-done.3, bf16[512,4096]{1,0:T(8,128)(2,1)} %refs_4_.5, bf16[256,4096]{1,0:T(8,128)(2,1)} %refs_5_.5, bf16[256,2048]{1,0:T(8,128)(2,1)} %refs_6_.5, ...), custom_call_target="tpu_custom_call" | custom-call | flops 17179869184 | bytes 16777216 | tf_op jit(solution)/shard_map/pallas_call | solution.py:287
Async XLA Ops:
  1.6 6.6 %collective-permute-start.3 = (bf16[1,144,512]{2,1,0:T(8,128)(2,1)}, bf16[1,144,512]{2,1,0:T(8,128)(2,1)S(1)}, u32[]{:S(2)}, u32[]{:S(2)}) collective-permute-start(bf16[1,144,512]{2,1,0:T(8,128)(2,1)} %bitcast.12), channel_id=1, source_target_pairs={{0,1},{1,0},{2,3},{3,2},{4,5},{5,4},{6,7},{7,6},{8,9},{9,8},{10,11... | collective-permute-start | bytes 442376 | tf_op jit(solution)/shard_map/ppermute | solution.py:320
  2.0 17.0 %collective-permute-start.2 = (bf16[144,512]{1,0:T(8,128)(2,1)}, bf16[144,512]{1,0:T(8,128)(2,1)S(1)}, u32[]{:S(2)}, u32[]{:S(2)}) collective-permute-start(bf16[144,512]{1,0:T(8,128)(2,1)} %shard_map.73), channel_id=1, source_target_pairs={{0,6},{2,8},{4,10},{6,12},{8,14},{10,16},{12,18},{14,20},{16,22},{... | collective-permute-start | bytes 442376 | tf_op jit(solution)/shard_map/ppermute | solution.py:21
  5.5 13.6 %collective-permute-start.1 = (bf16[144,512]{1,0:T(8,128)(2,1)}, bf16[144,512]{1,0:T(8,128)(2,1)S(1)}, u32[]{:S(2)}, u32[]{:S(2)}) collective-permute-start(bf16[144,512]{1,0:T(8,128)(2,1)} %shard_map.73), channel_id=1, source_target_pairs={{0,4},{2,6},{4,8},{6,10},{8,12},{10,14},{12,16},{14,18},{16,20},{1... | collective-permute-start | bytes 442376 | tf_op jit(solution)/shard_map/ppermute | solution.py:21
  7.0 13.4 %collective-permute-start = (bf16[144,512]{1,0:T(8,128)(2,1)}, bf16[144,512]{1,0:T(8,128)(2,1)S(1)}, u32[]{:S(2)}, u32[]{:S(2)}) collective-permute-start(bf16[144,512]{1,0:T(8,128)(2,1)} %shard_map.73), channel_id=1, source_target_pairs={{0,2},{2,4},{4,6},{6,8},{8,10},{10,12},{12,14},{14,16},{16,18},{18... | collective-permute-start | bytes 442376 | tf_op jit(solution)/shard_map/ppermute | solution.py:21
  8.2 12.4 %copy-start = (bf16[144,512]{1,0:T(8,128)(2,1)S(1)}, bf16[144,512]{1,0:T(8,128)(2,1)}, u32[]{:S(2)}) copy-start(bf16[144,512]{1,0:T(8,128)(2,1)} %shard_map.73) | copy-start | bytes 442372
  8.2 0.7 copy-start.5
  20.5 1.9 %copy-start.1 = (bf16[3,144,512]{2,1,0:T(8,128)(2,1)}, bf16[3,144,512]{2,1,0:T(8,128)(2,1)S(1)}, u32[]{:S(2)}) copy-start(bf16[3,144,512]{2,1,0:T(8,128)(2,1)S(1)} %pad_maximum_fusion.1.refs_2_) | copy-start | bytes 1327108
  20.5 1.9 %collective-permute-start.5 = (bf16[3,144,512]{2,1,0:T(8,128)(2,1)S(1)}, bf16[3,144,512]{2,1,0:T(8,128)(2,1)S(1)}, u32[]{:S(2)}, u32[]{:S(2)}) collective-permute-start(bf16[3,144,512]{2,1,0:T(8,128)(2,1)S(1)} %pad_maximum_fusion.1.refs_2_), channel_id=1, source_target_pairs={{0,1},{1,0},{2,3},{3,2},{4,5},{5,4},{6,7},{7,6},{8,9},{9,8},{10,11... | collective-permute-start | bytes 1327112 | tf_op jit(solution)/shard_map/ppermute | solution.py:320
  20.6 22.1 %collective-permute-start.4 = (bf16[4,144,512]{2,1,0:T(8,128)(2,1)S(1)}, bf16[4,144,512]{2,1,0:T(8,128)(2,1)S(1)}, u32[]{:S(2)}, u32[]{:S(2)}) collective-permute-start(bf16[4,144,512]{2,1,0:T(8,128)(2,1)S(1)} %pad_maximum_fusion), channel_id=1, source_target_pairs={{0,8},{2,10},{4,12},{6,14},{8,16},{10,18},{12,20},{14,22},{16,24},... | collective-permute-start | bytes 1769480 | tf_op jit(solution)/shard_map/ppermute | solution.py:21
  22.3 0.8 %copy-start.4 = (bf16[3,144,512]{2,1,0:T(8,128)(2,1)}, bf16[3,144,512]{2,1,0:T(8,128)(2,1)S(1)}, u32[]{:S(2)}) copy-start(bf16[3,144,512]{2,1,0:T(8,128)(2,1)S(1)} %collective-permute-done.5.refs_3_) | copy-start | bytes 1327108
  42.8 2.1 %copy-start.2 = (bf16[4,144,512]{2,1,0:T(8,128)(2,1)}, bf16[4,144,512]{2,1,0:T(8,128)(2,1)S(1)}, u32[]{:S(2)}) copy-start(bf16[4,144,512]{2,1,0:T(8,128)(2,1)S(1)} %collective-permute-done.4.refs_2_) | copy-start | bytes 1769476
  42.8 2.1 %collective-permute-start.6 = (bf16[4,144,512]{2,1,0:T(8,128)(2,1)S(1)}, bf16[4,144,512]{2,1,0:T(8,128)(2,1)S(1)}, u32[]{:S(2)}, u32[]{:S(2)}) collective-permute-start(bf16[4,144,512]{2,1,0:T(8,128)(2,1)S(1)} %collective-permute-done.4.refs_2_), channel_id=1, source_target_pairs={{0,1},{1,0},{2,3},{3,2},{4,5},{5,4},{6,7},{7,6},{8,9},{9,8},{10,11... | collective-permute-start | bytes 1769480 | tf_op jit(solution)/shard_map/ppermute | solution.py:320
  44.9 0.8 %copy-start.3 = (bf16[4,144,512]{2,1,0:T(8,128)(2,1)}, bf16[4,144,512]{2,1,0:T(8,128)(2,1)S(1)}, u32[]{:S(2)}) copy-start(bf16[4,144,512]{2,1,0:T(8,128)(2,1)S(1)} %collective-permute-done.6.refs_3_) | copy-start | bytes 1769476
